TPU v7x, 32 devices: a whole 2x2x4 slice. The times are simulated.
32 devices in a mesh: dp: 8 (over z, y), tensor: 4 (over x, core).
Axes of the slice: x: 2, y: 2, z: 4, core: 2. Of those that a mesh axis runs over, the one named last changes fastest.
Arguments:
- inputs: bfloat16 [6304, 768], P(('dp', 'tensor')), may hold values from -6 to 6
- cotangent: bfloat16 [6304, 768], P(('dp', 'tensor')), may hold values from -6 to 6
- expert_ids: int32 [6304, 2], P('dp'), may hold values from 0 to 15, all different within a row; in each aligned block of 788 rows (0 to 787, 788 to 1575, ...) at most 147 rows name the same one
- layer_norm_gains: float32 [2, 768], replicated, may hold values from 0.5 to 1.5
- layer_norm_biases: float32 [2, 768], replicated, may hold values from -1.2 to 1.2
- norm_moment: float32 [4, 768], replicated, may hold values from -512 to 512
- w_qkv: bfloat16 [3, 768, 768], P(None, 'dp', 'tensor'), may hold values from -0.21875 to 0.21875
- w_attn_out: bfloat16 [768, 768], P('tensor', 'dp'), may hold values from -1.25 to 1.25
- w_router: bfloat16 [768, 16], replicated, may hold values from -0.21875 to 0.21875
- w_in: bfloat16 [16, 768, 3072], P(None, 'dp', 'tensor'), may hold values from -0.21875 to 0.21875
- w_exp_out: bfloat16 [16, 3072, 768], P(None, 'tensor', 'dp'), may hold values from -0.625 to 0.625
- m_qkv: float32 [3, 768, 768], P(None, 'dp', 'tensor'), may hold values from -512 to 512
- m_attn_out: float32 [768, 768], P('tensor', 'dp'), may hold values from -96 to 96
- m_router: float32 [768, 16], replicated, may hold values from -1024 to 1024
- m_in: float32 [16, 768, 3072], P(None, 'dp', 'tensor'), may hold values from -32 to 32
- m_exp_out: float32 [16, 3072, 768], P(None, 'tensor', 'dp'), may hold values from -6 to 6
Outputs:
- output: bfloat16 [6304, 768], P(('dp', 'tensor'))
- input_grad: float32 [6304, 768], P(('dp', 'tensor'))
- norm_moment_new: float32 [4, 768], replicated
- norm_new: float32 [4, 768], replicated
- qkv_moment_new: float32 [3, 768, 768], P(None, 'dp', 'tensor')
- qkv_new: float32 [3, 768, 768], P(None, 'dp', 'tensor')
- attn_out_moment_new: float32 [768, 768], P('tensor', 'dp')
- attn_out_new: float32 [768, 768], P('tensor', 'dp')
- router_moment_new: float32 [768, 16], replicated
- router_new: float32 [768, 16], replicated
- in_moment_new: float32 [16, 768, 3072], P(None, 'dp', 'tensor')
- in_new: float32 [16, 768, 3072], P(None, 'dp', 'tensor')
- exp_out_moment_new: float32 [16, 3072, 768], P(None, 'tensor', 'dp')
- exp_out_new: float32 [16, 3072, 768], P(None, 'tensor', 'dp')
Inputs may be any that keep to these rules, and one draw needn't show every extreme that they name: `expert_ids`: within each aligned block of 788 rows (the tokens of one index of dp) no expert is named by more than 147 rows, a bound that some block reaches; the 2 ids of a row differ.
All inputs are finite; a program needn't handle non-finite values.
Results may differ from a plain program's by a relative error of at most 0.018.
Values may be sent and summed in bfloat16 or wider, within the bound.
A program may use at most 320 MiB of HBM per device.

v0:
```python
import math

import jax
import jax.numpy as jnp
import numpy as np
from jax import lax
from jax.sharding import PartitionSpec as P

D = 768
HD = 64
FF = 3072
IMGS = 4
CAP = 147


HIGH = lax.Precision.HIGHEST
LN_EPS = 1e-06
NS_EPS = 1e-07
NS_A = 3.4445
NS_B = -4.775
NS_C = 2.0315
DECAY = 0.5
VEC_RATE = 0.0002
INV_ROOT_TWO = 0.7071067811865476
INV_ROOT_TWO_PI = 0.3989422804014327


def shortened(x):

    def short(part):
        return part.astype(jnp.bfloat16) if part.dtype == jnp.float32 else part

    return jax.tree.map(short, x)


def apply_layer_norm(values, gain_row, offset_row):
    centre = values - jnp.mean(values, axis=-1, keepdims=True)
    inv_std = lax.rsqrt(jnp.mean(centre * centre, axis=-1, keepdims=True) + LN_EPS)
    normed = centre * inv_std
    return (normed * gain_row + offset_row, normed, inv_std)


def norm_back(grad_normed, normed, inv_std, gain_row):
    scaled = grad_normed * gain_row
    first_mean = jnp.mean(scaled, axis=-1, keepdims=True)
    second_mean = jnp.mean(scaled * normed, axis=-1, keepdims=True)
    grad_values = inv_std * (scaled - first_mean - normed * second_mean)
    return (grad_values, jnp.sum(grad_normed * normed, axis=0), jnp.sum(grad_normed, axis=0))


def gelu_slope(values):
    return (
        0.5 * (1.0 + lax.erf(values * INV_ROOT_TWO))
        + values * jnp.exp(-0.5 * values * values) * INV_ROOT_TWO_PI
    )


def route_slots(picked, experts, capacity):
    flat_ids = picked.reshape(-1)
    entries = flat_ids.shape[0]
    labels = lax.broadcasted_iota(jnp.int32, (entries, experts), 1)
    onehot = (flat_ids[:, None] == labels).astype(jnp.int32)
    running = jnp.cumsum(onehot, axis=0) - 1
    places = jnp.sum(running * onehot, axis=1)
    target_slot = flat_ids * capacity + places
    sources = (
        jnp.full((experts * capacity,), entries, jnp.int32)
        .at[target_slot]
        .set(jnp.arange(entries, dtype=jnp.int32))
    )
    return (target_slot, sources)


def gather_rows(local_rows):
    return lax.all_gather(local_rows, "tensor", axis=0, tiled=True)


def reduce_rows(partial_rows):
    return lax.psum_scatter(partial_rows, "tensor", scatter_dimension=0, tiled=True)


def gram(blocks):
    return lax.psum(
        jnp.einsum("kic,kjc->kij", blocks, blocks, precision=HIGH).astype(jnp.bfloat16), "tensor"
    ).astype(jnp.float32)


def split_heads(qkv_all, images, head_size):
    return qkv_all.reshape(qkv_all.shape[0], images, -1, qkv_all.shape[2] // head_size, head_size)


def local_orthogonalize(matrix):
    norm_value = jnp.sqrt(jnp.sum(matrix * matrix))
    current = matrix / (norm_value + NS_EPS)
    for repeat in range(5):
        square = jnp.dot(current, current.T, precision=HIGH)
        poly_term = NS_B * square + NS_C * jnp.dot(square, square, precision=HIGH)
        current = NS_A * current + jnp.dot(poly_term, current, precision=HIGH)
    return current


def widen(blocks, slot_width):
    return jnp.pad(blocks, ((0, 0), (0, 0), (0, slot_width - blocks.shape[2])))


def local(
    inputs,
    cotangent,
    expert_ids,
    layer_norm_gains,
    layer_norm_biases,
    norm_moment,
    w_qkv,
    w_attn_out,
    w_router,
    w_in,
    w_exp_out,
    m_qkv,
    m_attn_out,
    m_router,
    m_in,
    m_exp_out,
):
    rows_local = inputs.shape[0]
    group_rows = expert_ids.shape[0]
    top_count = expert_ids.shape[1]
    experts = w_in.shape[0]
    capacity = CAP
    images = IMGS
    scale_qk = HD ** (-0.5)
    model_width = inputs.shape[1]
    dp_count = lax.axis_size("dp")
    per_host = max(1, experts // dp_count)
    copies = max(1, dp_count // experts)
    row_share = w_in.shape[1]
    part_cols = w_in.shape[2] // copies
    hosted = np.arange(dp_count * per_host).reshape(dp_count, per_host) // copies
    replica = (np.arange(dp_count) % copies)[:, None]
    full_qkv, full_out = (
        lax.all_gather(w_qkv, "dp", axis=1, tiled=True),
        lax.all_gather(w_attn_out, "dp", axis=1, tiled=True),
    )
    hidden_input_rows = inputs.astype(jnp.float32)
    first_normalized, first_centered_scaled, first_inverse_deviation = apply_layer_norm(
        hidden_input_rows, layer_norm_gains[0], layer_norm_biases[0]
    )
    rows_one = gather_rows(first_normalized.astype(jnp.bfloat16))
    qkv_all = jnp.einsum(
        "td,sde->ste", rows_one, full_qkv, preferred_element_type=jnp.float32
    ).astype(jnp.bfloat16)
    stacked = split_heads(qkv_all, images, HD)
    scores = (
        jnp.einsum("bqhe,bkhe->bhqk", stacked[0], stacked[1], preferred_element_type=jnp.float32)
        * scale_qk
    )
    row_max = jnp.max(scores, axis=-1, keepdims=True)
    expo = jnp.exp(scores - row_max)
    denom = jnp.sum(expo, axis=-1, keepdims=True)
    probs = expo / denom
    log_total = row_max + jnp.log(denom)
    mixed = jnp.einsum(
        "bhqk,bkhe->bqhe",
        probs.astype(jnp.bfloat16),
        stacked[2],
        preferred_element_type=jnp.float32,
    )
    mixed = mixed.astype(jnp.bfloat16).reshape(group_rows, -1)
    attended = reduce_rows(jnp.dot(mixed, full_out, preferred_element_type=jnp.float32))
    residual_midpoint = hidden_input_rows + attended
    second_normalized, second_centered_scaled, second_inverse_deviation = apply_layer_norm(
        residual_midpoint, layer_norm_gains[1], layer_norm_biases[1]
    )
    act_two = second_normalized.astype(jnp.bfloat16)
    rows_two = gather_rows(act_two)
    logits = jnp.dot(rows_two, w_router, preferred_element_type=jnp.float32)
    router_probs = jax.nn.softmax(logits, axis=-1)
    labels = lax.broadcasted_iota(jnp.int32, (group_rows, top_count, experts), 2)
    chosen = (expert_ids[:, :, None] == labels).astype(jnp.float32)
    gates = jnp.sum(router_probs[:, None, :] * chosen, axis=2)
    target_slot, sources = route_slots(expert_ids, experts, capacity)
    pair_count = group_rows * top_count
    token_of_slot = jnp.where(sources < pair_count, sources // top_count, group_rows)
    gate_flat = jnp.concatenate([gates.reshape(-1), jnp.zeros((1,), jnp.float32)])
    gate_of_slot = gate_flat[sources]
    padded_rows = jnp.concatenate([rows_two, jnp.zeros((1, model_width), jnp.bfloat16)], 0)
    expert_rows = padded_rows[token_of_slot].reshape(experts, capacity, model_width)
    in_parts = w_in.reshape(experts, row_share, copies, part_cols).transpose(0, 2, 1, 3)[
        hosted, replica
    ]
    exp_parts = w_exp_out.reshape(experts, copies, part_cols, row_share).transpose(0, 1, 3, 2)[
        hosted, replica
    ]
    slot_parts = expert_rows[hosted]
    got_rows, got_in, got_exp = (
        lax.all_to_all(slot_parts, "dp", split_axis=0, concat_axis=2, tiled=True),
        lax.all_to_all(in_parts, "dp", split_axis=0, concat_axis=2, tiled=True),
        lax.all_to_all(exp_parts, "dp", split_axis=0, concat_axis=2, tiled=True),
    )
    host_rows = got_rows[0]
    host_in = got_in[0]
    host_exp = got_exp[0]
    host_pre = jnp.einsum("ecd,edf->ecf", host_rows, host_in, preferred_element_type=jnp.float32)
    host_act = jax.nn.gelu(host_pre, approximate=False).astype(jnp.bfloat16)
    host_out = jnp.einsum("ecf,edf->ecd", host_act, host_exp, preferred_element_type=jnp.float32)
    came_back = lax.all_to_all(host_out, "dp", split_axis=1, concat_axis=0, tiled=True)
    expert_out = jnp.sum(came_back.reshape(experts, copies, capacity, model_width), axis=1).reshape(
        experts * capacity, model_width
    )
    picked_out = expert_out[target_slot].reshape(group_rows, top_count, model_width)
    combined = jnp.sum(gates[:, :, None] * picked_out, axis=1)
    moe_local = reduce_rows(combined)
    output = (residual_midpoint + moe_local).astype(jnp.bfloat16)
    back_qkv, back_out = (
        lax.all_gather(w_qkv, "dp", axis=1, tiled=True),
        lax.all_gather(w_attn_out, "dp", axis=1, tiled=True),
    )
    grad_output = cotangent.astype(jnp.float32)
    grad_rows = gather_rows(cotangent).astype(jnp.float32)
    padded_grad = jnp.concatenate([grad_rows, jnp.zeros((1, model_width), jnp.float32)], 0)
    grad_at_slot = padded_grad[token_of_slot]
    grad_slot = (
        (gate_of_slot[:, None] * grad_at_slot)
        .astype(jnp.bfloat16)
        .reshape(experts, capacity, model_width)
    )
    grad_gate_slot = jnp.concatenate(
        [jnp.sum(grad_at_slot * expert_out, axis=1), jnp.zeros((1,), jnp.float32)]
    )
    grad_gate_part = grad_gate_slot[target_slot].reshape(group_rows, top_count)
    host_grad = lax.all_to_all(grad_slot[hosted], "dp", split_axis=0, concat_axis=2, tiled=True)[0]
    host_grad_act = jnp.einsum(
        "ecd,edf->ecf", host_grad, host_exp, preferred_element_type=jnp.float32
    )
    host_grad_pre = (host_grad_act * gelu_slope(host_pre)).astype(jnp.bfloat16)
    host_exp_grad = jnp.einsum(
        "ecd,ecf->edf", host_grad, host_act, preferred_element_type=jnp.float32
    )
    host_in_grad = jnp.einsum(
        "ecd,ecf->edf", host_rows, host_grad_pre, preferred_element_type=jnp.float32
    )
    host_row_grad = jnp.einsum(
        "ecf,edf->ecd", host_grad_pre, host_in, preferred_element_type=jnp.float32
    )
    back_rows, back_in_grad, back_exp_grad = (
        lax.all_to_all(host_row_grad, "dp", split_axis=1, concat_axis=0, tiled=True),
        lax.all_to_all(host_in_grad, "dp", split_axis=1, concat_axis=0, tiled=True),
        lax.all_to_all(host_exp_grad, "dp", split_axis=1, concat_axis=0, tiled=True),
    )
    grad_rows_exp = jnp.sum(
        back_rows.reshape(experts, copies, capacity, model_width), axis=1
    ).reshape(experts * capacity, model_width)
    red_in = (
        back_in_grad.reshape(experts, copies, row_share, part_cols)
        .transpose(0, 2, 1, 3)
        .reshape(experts, row_share, copies * part_cols)
    )
    red_exp = (
        back_exp_grad.reshape(experts, copies, row_share, part_cols)
        .transpose(0, 1, 3, 2)
        .reshape(experts, copies * part_cols, row_share)
    )
    grad_two_part = jnp.sum(
        grad_rows_exp[target_slot].reshape(group_rows, top_count, model_width), axis=1
    )
    grad_two_local, grad_gate_local = (
        lax.psum_scatter(grad_two_part, "tensor", scatter_dimension=0, tiled=True),
        lax.psum_scatter(grad_gate_part, "tensor", scatter_dimension=0, tiled=True),
    )
    start = lax.axis_index("tensor") * rows_local
    probs_local = lax.dynamic_slice_in_dim(router_probs, start, rows_local, 0)
    chosen_local = lax.dynamic_slice_in_dim(chosen, start, rows_local, 0)
    grad_probs = jnp.sum(grad_gate_local[:, :, None] * chosen_local, axis=1)
    grad_logits = (
        probs_local * (grad_probs - jnp.sum(probs_local * grad_probs, axis=-1, keepdims=True))
    ).astype(jnp.bfloat16)
    second_norm_gradient = grad_two_local + jnp.einsum(
        "te,de->td", grad_logits, w_router, preferred_element_type=jnp.float32
    )
    router_part = jnp.einsum("td,te->de", act_two, grad_logits, preferred_element_type=jnp.float32)
    grad_mid_norm, gain_two_grad, bias_two_grad = norm_back(
        second_norm_gradient, second_centered_scaled, second_inverse_deviation, layer_norm_gains[1]
    )
    grad_middle = grad_mid_norm + grad_output
    grad_attn_rows = gather_rows(grad_middle.astype(jnp.bfloat16))
    grad_mixed = jnp.einsum(
        "td,ed->te", grad_attn_rows, back_out, preferred_element_type=jnp.float32
    ).astype(jnp.bfloat16)
    grad_out_w = jnp.einsum("te,td->ed", mixed, grad_attn_rows, preferred_element_type=jnp.float32)
    again_scores = (
        jnp.einsum("bqhe,bkhe->bhqk", stacked[0], stacked[1], preferred_element_type=jnp.float32)
        * scale_qk
    )
    again_probs = jnp.exp(again_scores - log_total)
    grad_mixed_heads = grad_mixed.reshape(stacked.shape[1:])
    grad_weights = jnp.einsum(
        "bqhe,bkhe->bhqk", grad_mixed_heads, stacked[2], preferred_element_type=jnp.float32
    )
    delta = jnp.sum(again_probs * grad_weights, axis=-1, keepdims=True)
    grad_scores = (again_probs * (grad_weights - delta)).astype(jnp.bfloat16)
    grad_query = (
        jnp.einsum("bhqk,bkhe->bqhe", grad_scores, stacked[1], preferred_element_type=jnp.float32)
        * scale_qk
    ).astype(jnp.bfloat16)
    grad_key = (
        jnp.einsum("bhqk,bqhe->bkhe", grad_scores, stacked[0], preferred_element_type=jnp.float32)
        * scale_qk
    ).astype(jnp.bfloat16)
    grad_value = jnp.einsum(
        "bhqk,bqhe->bkhe",
        again_probs.astype(jnp.bfloat16),
        grad_mixed_heads,
        preferred_element_type=jnp.float32,
    ).astype(jnp.bfloat16)
    grad_qkv = jnp.stack([grad_query, grad_key, grad_value]).reshape(qkv_all.shape)
    grad_qkv_w = jnp.einsum("td,ste->sde", rows_one, grad_qkv, preferred_element_type=jnp.float32)
    first_norm_gradient = reduce_rows(
        jnp.einsum("ste,sde->td", grad_qkv, back_qkv, preferred_element_type=jnp.float32)
    )
    grad_in_norm, gain_one_grad, bias_one_grad = norm_back(
        first_norm_gradient, first_centered_scaled, first_inverse_deviation, layer_norm_gains[0]
    )
    input_grad = grad_in_norm + grad_middle
    red_qkv, red_out = (
        lax.psum_scatter(grad_qkv_w, "dp", scatter_dimension=1, tiled=True),
        lax.psum_scatter(grad_out_w, "dp", scatter_dimension=1, tiled=True),
    )
    vec_part = jnp.stack([gain_one_grad, gain_two_grad, bias_one_grad, bias_two_grad])
    vec_grad, router_grad = lax.psum((vec_part, router_part), ("dp", "tensor"))
    norm_moment_new = DECAY * norm_moment + vec_grad
    norm_new = (
        jnp.concatenate([layer_norm_gains, layer_norm_biases], 0) - VEC_RATE * norm_moment_new
    )
    router_moment_new = DECAY * m_router + router_grad
    router_new = w_router.astype(jnp.float32) - local_orthogonalize(router_moment_new.T).T
    qkv_moment_new = DECAY * m_qkv + red_qkv
    attn_out_moment_new = DECAY * m_attn_out + red_out
    in_moment_new = DECAY * m_in + red_in
    exp_out_moment_new = DECAY * m_exp_out + red_exp
    shard_rows = in_moment_new.shape[1]
    hidden_cols = in_moment_new.shape[2]
    head_cols = attn_out_moment_new.shape[0]
    slot_width = max(hidden_cols, 3 * head_cols)
    matrices = 2 * experts + 2
    per_owner = (matrices + dp_count - 1) // dp_count
    packed = jnp.concatenate(
        [
            widen(in_moment_new, slot_width),
            widen(jnp.swapaxes(exp_out_moment_new, 1, 2), slot_width),
            widen(
                qkv_moment_new.transpose(1, 0, 2).reshape(1, shard_rows, 3 * head_cols), slot_width
            ),
            widen(attn_out_moment_new.T[None], slot_width),
        ],
        0,
    )
    packed = jnp.pad(packed, ((0, per_owner * dp_count - matrices), (0, 0), (0, 0)))
    outgoing = packed.reshape(dp_count, per_owner, shard_rows, slot_width)
    owned = lax.all_to_all(outgoing, "dp", split_axis=0, concat_axis=2, tiled=True)[0]
    square = gram(owned)
    diag_sum = jnp.sum(jnp.diagonal(square, axis1=1, axis2=2), axis=1)
    inverse = 1.0 / (jnp.sqrt(diag_sum) + NS_EPS)
    orthogonal = owned * inverse[:, None, None]
    square = square * (inverse * inverse)[:, None, None]
    for repeat in range(5):
        poly_term = NS_B * square + NS_C * jnp.einsum(
            "kij,kjl->kil", square, square, precision=HIGH
        )
        orthogonal = NS_A * orthogonal + jnp.einsum(
            "kij,kjc->kic", poly_term, orthogonal, precision=HIGH
        )
        if repeat < 4:
            square = gram(orthogonal)
    returned = lax.all_to_all(
        shortened(orthogonal[None]), "dp", split_axis=2, concat_axis=0, tiled=True
    )
    unpacked = returned.reshape(dp_count * per_owner, shard_rows, slot_width)
    ortho_in = unpacked[:experts, :, :hidden_cols]
    ortho_exp = jnp.swapaxes(unpacked[experts : 2 * experts, :, :hidden_cols], 1, 2)
    ortho_qkv = (
        unpacked[2 * experts, :, : 3 * head_cols]
        .reshape(shard_rows, 3, head_cols)
        .transpose(1, 0, 2)
    )
    ortho_out = unpacked[2 * experts + 1, :, :head_cols].T
    qkv_new = w_qkv.astype(jnp.float32) - math.sqrt(3.0) * ortho_qkv
    attn_out_new = w_attn_out.astype(jnp.float32) - ortho_out
    in_new = w_in.astype(jnp.float32) - math.sqrt(max(1.0, FF / D)) * ortho_in
    exp_out_new = w_exp_out.astype(jnp.float32) - ortho_exp
    return (
        output,
        input_grad,
        norm_moment_new,
        norm_new,
        qkv_moment_new,
        qkv_new,
        attn_out_moment_new,
        attn_out_new,
        router_moment_new,
        router_new,
        in_moment_new,
        in_new,
        exp_out_moment_new,
        exp_out_new,
    )


def solution(mesh):
    in_specs = (
        P(("dp", "tensor"), None),
        P(("dp", "tensor"), None),
        P("dp", None),
        P(),
        P(),
        P(),
        P(None, "dp", "tensor"),
        P("tensor", "dp"),
        P(),
        P(None, "dp", "tensor"),
        P(None, "tensor", "dp"),
        P(None, "dp", "tensor"),
        P("tensor", "dp"),
        P(),
        P(None, "dp", "tensor"),
        P(None, "tensor", "dp"),
    )
    out_specs = (
        P(("dp", "tensor"), None),
        P(("dp", "tensor"), None),
        P(),
        P(),
        P(None, "dp", "tensor"),
        P(None, "dp", "tensor"),
        P("tensor", "dp"),
        P("tensor", "dp"),
        P(),
        P(),
        P(None, "dp", "tensor"),
        P(None, "dp", "tensor"),
        P(None, "tensor", "dp"),
        P(None, "tensor", "dp"),
    )
    return jax.shard_map(local, mesh=mesh, in_specs=in_specs, out_specs=out_specs, check_vma=False)
```

profile of v0, /device:TPU:0, one launch (start us, length us, event | category | flops | bytes accessed | tf_op | source)
XLA Modules:
  0.0 2655.2 jit_solution(9982365186979433122)
XLA Ops:
  20.1 80.6 %all_gather.21 = bf16[3,768,192]{2,0,1:T(4,128)(2,1)} all-gather(bf16[3,96,192]{2,0,1:T(4,128)(2,1)S(1)} %copy.226), channel_id=1, replica_groups=mesh['dp'=8,'tensor'=4] {'dp'}, dimensions={1}, use_global_device_ids=true | all-gather | bytes 995328 | tf_op jit(solution)/shard_map/all_gather | solution.py:140
  106.4 31.1 %all_gather.22 = bf16[192,768]{0,1:T(8,128)(2,1)S(1)} all-gather(bf16[192,96]{0,1:T(8,128)(2,1)S(1)} %copy.233), channel_id=1, replica_groups=mesh['dp'=8,'tensor'=4] {'dp'}, dimensions={1}, use_global_device_ids=true | all-gather | bytes 331776 | tf_op jit(solution)/shard_map/all_gather | solution.py:141
  152.6 25.6 fusion
  192.0 9.0 scatter_custom_fusion
  209.4 8.4 gather_fusion
  239.3 19.9 all-gather.13.cloned.1.call-done
  278.9 12.7 gather_fusion.5
  331.7 16.7 fusion.41
  351.6 8.5 copy.241
  360.1 44.8 %all-to-all-done.4 = bf16[8,2,147,768]{3,1,2,0:T(2,128)(2,1)} async-done(((bf16[8,2,147,768]{3,1,2,0:T(2,128)(2,1)}), bf16[8,2,147,768]{3,1,2,0:T(2,128)(2,1)}, u32[]{:S(2)}, u32[]{:S(2)}) %all-to-all-start.4) | async-done | bytes 3612704 | tf_op jit(solution)/shard_map/all_to_all | solution.py:230
  421.4 8.5 copy.247
  429.9 137.3 %all-to-all-done.3 = f32[2,1176,768]{2,0,1:T(2,128)} async-done(((f32[2,1176,768]{2,0,1:T(2,128)}), f32[2,1176,768]{2,0,1:T(2,128)}, u32[]{:S(2)}, u32[]{:S(2)}) %all-to-all-start.3) | async-done | bytes 7225376 | tf_op jit(solution)/shard_map/all_to_all | solution.py:205
  584.7 144.6 %all-to-all-done.5 = f32[2,1176,768]{2,0,1:T(2,128)} async-done(((f32[2,1176,768]{2,0,1:T(2,128)}), f32[2,1176,768]{2,0,1:T(2,128)}, u32[]{:S(2)}, u32[]{:S(2)}) %all-to-all-start.5) | async-done | bytes 7225376 | tf_op jit(solution)/shard_map/all_to_all | solution.py:245
  747.2 8.8 gather_fusion.9
  768.7 10.5 gather_fusion.8
  794.3 28.5 %fusion.173 = (f32[208,2]{1,0:T(8,128)S(1)}, f32[200,768]{1,0:T(8,128)}) fusion(f32[788,2]{1,0:T(8,128)S(1)} %reshape.258, f32[788,768]{1,0:T(8,128)S(1)} %reduce_sum.238), kind=kCustom, calls=%all-reduce-scatter.6 | all-reduce-scatter fusion | flops 616066 | bytes 3043616
  867.8 15.4 all-gather.15.cloned.1.call-done
  923.2 38.6 %all-to-all-done.6 = f32[2,768,768]{2,0,1:T(2,128)} async-done(((f32[2,768,768]{2,0,1:T(2,128)}), f32[2,768,768]{2,0,1:T(2,128)}, u32[]{:S(2)}, u32[]{:S(2)}) %all-to-all-start.6) | async-done | bytes 4718624 | tf_op jit(solution)/shard_map/all_to_all | solution.py:246
  973.8 19.0 reduce-scatter.19.cloned.1.call-done
  993.9 68.5 %reduce-scatter.17.cloned.1.call-done = f32[96,576]{1,0:T(8,128)} async-done(((f32[768,576]{1,0:T(8,128)}), f32[96,576]{1,0:T(8,128)}) %reduce-scatter.17.cloned.1.call-update) | async-done | bytes 221200
  1064.4 8.9 select_maximum_fusion
  1078.5 258.5 %all_to_all.153 = f32[8,5,96,768]{3,2,1,0:T(8,128)} all-to-all(f32[8,5,96,768]{3,2,1,0:T(8,128)S(1)} %bitcast.260), channel_id=1, replica_groups=mesh['dp'=8,'tensor'=4] {'dp'}, dimensions={0} | all-to-all | bytes 23592960 | tf_op jit(solution)/shard_map/all_to_all | solution.py:358
  1337.1 10.0 copy.273
  1347.1 34.0 %convolution_convert_fusion.4 = bf16[5,768,768]{2,1,0:T(8,128)(2,1)} fusion(f32[5,768,768]{2,1,0:T(8,128)} %bitcast.256), kind=kOutput, calls=%fused_computation.110 | convolution fusion | flops 27182039040 | bytes 17694720 | tf_op jit(solution)/shard_map/kic,kjc->kij/dot_general | solution.py:84
  1381.4 112.0 %all-reduce.25.cloned.1.call-done = bf16[5,768,768]{2,1,0:T(8,128)(2,1)} async-done(((bf16[5,768,768]{2,1,0:T(8,128)(2,1)}), bf16[5,768,768]{2,1,0:T(8,128)(2,1)}) %all-reduce.25.cloned.1.call-update) | async-done | bytes 5898256 | tf_op jit(solution)/shard_map/psum | solution.py:83
  1493.3 12.7 copy.274
  1513.4 34.2 %fusion.29 = f32[5,768,768]{2,1,0:T(8,128)} fusion(f32[5]{0:T(128)S(1)} %get-tuple-element.112, bf16[5,768,768]{2,1,0:T(8,128)(2,1)} %all-reduce.25.cloned.1.call-done), kind=kOutput, calls=%fused_computation.43 | convolution fusion | flops 27184988160 | bytes 17694740 | tf_op jit(solution)/shard_map/kij,kjl->kil/dot_general | solution.py:365
  1547.6 34.3 %multiply_add_fusion.3 = f32[5,768,768]{2,1,0:T(8,128)S(1)} fusion(f32[5,768,768]{2,1,0:T(8,128)S(1)} %bitcast.259, f32[5,768,768]{2,1,0:T(8,128)} %fusion.29, f32[5]{0:T(128)S(1)} %get-tuple-element.112, f32[5]{0:T(128)S(1)} %get-tuple-element.113, bf16[5,768,768]{2,1,0:T(8,128)(2,1)} %all-reduce.25.cloned.1.call-done), kind=kOutput, calls=%fused_computation.42 | convolution fusion | flops 27205632000 | bytes 41287720 | tf_op jit(solution)/shard_map/kij,kjc->kic/dot_general | solution.py:368
  1586.2 30.5 %convolution_convert_fusion.3 = bf16[5,768,768]{2,1,0:T(8,128)(2,1)} fusion(f32[5,768,768]{2,1,0:T(8,128)S(1)} %multiply_add_fusion.3), kind=kOutput, calls=%fused_computation.109 | convolution fusion | flops 27182039040 | bytes 17694720 | tf_op jit(solution)/shard_map/kic,kjc->kij/dot_general | solution.py:84
  1616.8 113.5 %all-reduce.27.cloned.1.call-done = bf16[5,768,768]{2,1,0:T(8,128)(2,1)} async-done(((bf16[5,768,768]{2,1,0:T(8,128)(2,1)}), bf16[5,768,768]{2,1,0:T(8,128)(2,1)}) %all-reduce.27.cloned.1.call-update) | async-done | bytes 5898256 | tf_op jit(solution)/shard_map/psum | solution.py:83
  1730.3 9.6 fusion.182
  1739.9 34.7 %multiply_add_fusion.2 = f32[5,768,768]{2,1,0:T(8,128)S(1)} fusion(f32[5,768,768]{2,1,0:T(8,128)} %copy-done, f32[5,768,768]{2,1,0:T(8,128)S(1)} %fusion.182, bf16[5,768,768]{2,1,0:T(8,128)(2,1)S(1)} %copy-done.19), kind=kOutput, calls=%fused_computation.37 | convolution fusion | flops 27196784640 | bytes 41287680 | tf_op jit(solution)/shard_map/kij,kjc->kic/dot_general | solution.py:368
  1778.9 30.6 %convolution_convert_fusion.2 = bf16[5,768,768]{2,1,0:T(8,128)(2,1)} fusion(f32[5,768,768]{2,1,0:T(8,128)S(1)} %multiply_add_fusion.2), kind=kOutput, calls=%fused_computation.108 | convolution fusion | flops 27182039040 | bytes 17694720 | tf_op jit(solution)/shard_map/kic,kjc->kij/dot_general | solution.py:84
  1809.6 113.5 %all-reduce.29.cloned.1.call-done = bf16[5,768,768]{2,1,0:T(8,128)(2,1)} async-done(((bf16[5,768,768]{2,1,0:T(8,128)(2,1)}), bf16[5,768,768]{2,1,0:T(8,128)(2,1)}) %all-reduce.29.cloned.1.call-update) | async-done | bytes 5898256 | tf_op jit(solution)/shard_map/psum | solution.py:83
  1923.1 9.7 fusion.183
  1932.8 34.7 %multiply_add_fusion.1 = f32[5,768,768]{2,1,0:T(8,128)S(1)} fusion(f32[5,768,768]{2,1,0:T(8,128)} %copy-done.1, f32[5,768,768]{2,1,0:T(8,128)S(1)} %fusion.183, bf16[5,768,768]{2,1,0:T(8,128)(2,1)S(1)} %copy-done.20), kind=kOutput, calls=%fused_computation.31 | convolution fusion | flops 27196784640 | bytes 41287680 | tf_op jit(solution)/shard_map/kij,kjc->kic/dot_general | solution.py:368
  1971.8 30.9 %convolution_convert_fusion.1 = bf16[5,768,768]{2,1,0:T(8,128)(2,1)} fusion(f32[5,768,768]{2,1,0:T(8,128)S(1)} %multiply_add_fusion.1), kind=kOutput, calls=%fused_computation.107 | convolution fusion | flops 27182039040 | bytes 17694720 | tf_op jit(solution)/shard_map/kic,kjc->kij/dot_general | solution.py:84
  2002.8 113.5 %all-reduce.31.cloned.1.call-done = bf16[5,768,768]{2,1,0:T(8,128)(2,1)} async-done(((bf16[5,768,768]{2,1,0:T(8,128)(2,1)}), bf16[5,768,768]{2,1,0:T(8,128)(2,1)}) %all-reduce.31.cloned.1.call-update) | async-done | bytes 5898256 | tf_op jit(solution)/shard_map/psum | solution.py:83
  2116.2 9.6 fusion.184
  2125.8 34.7 %multiply_add_fusion = f32[5,768,768]{2,1,0:T(8,128)S(1)} fusion(f32[5,768,768]{2,1,0:T(8,128)} %copy-done.2, f32[5,768,768]{2,1,0:T(8,128)S(1)} %fusion.184, bf16[5,768,768]{2,1,0:T(8,128)(2,1)S(1)} %copy-done.21), kind=kOutput, calls=%fused_computation.25 | convolution fusion | flops 27196784640 | bytes 41287680 | tf_op jit(solution)/shard_map/kij,kjc->kic/dot_general | solution.py:368
  2164.8 30.6 %convolution_convert_fusion = bf16[5,768,768]{2,1,0:T(8,128)(2,1)} fusion(f32[5,768,768]{2,1,0:T(8,128)S(1)} %multiply_add_fusion), kind=kOutput, calls=%fused_computation.106 | convolution fusion | flops 27182039040 | bytes 17694720 | tf_op jit(solution)/shard_map/kic,kjc->kij/dot_general | solution.py:84
  2195.4 113.5 %all-reduce.33.cloned.1.call-done = bf16[5,768,768]{2,1,0:T(8,128)(2,1)} async-done(((bf16[5,768,768]{2,1,0:T(8,128)(2,1)}), bf16[5,768,768]{2,1,0:T(8,128)(2,1)}) %all-reduce.33.cloned.1.call-update) | async-done | bytes 5898256 | tf_op jit(solution)/shard_map/psum | solution.py:83
  2308.9 13.5 fusion.185
  2322.5 36.2 %fusion.54 = bf16[1,5,768,768]{3,2,1,0:T(8,128)(2,1)S(1)} fusion(f32[5,768,768]{2,1,0:T(8,128)} %copy-done.3, f32[5,768,768]{2,1,0:T(8,128)} %fusion.185, bf16[5,768,768]{2,1,0:T(8,128)(2,1)} %all-reduce.33.cloned.1.call-done), kind=kOutput, calls=%fused_computation.87 | convolution fusion | flops 27199733760 | bytes 35389440 | tf_op jit(solution)/shard_map/kij,kjc->kic/dot_general | solution.py:368
  2392.6 10.5 gather_fusion.4
  2422.7 45.9 %fusion.172 = (f32[200,768]{1,0:T(8,128)}, f32[200,768]{1,0:T(8,128)}) fusion(f32[788,768]{1,0:T(8,128)S(1)} %multiply_reduce_fusion, f32[788,768]{1,0:T(8,128)} %convolution_bitcast_fusion), kind=kCustom, calls=%all-reduce-scatter.5 | all-reduce-scatter fusion | flops 1228801 | bytes 6070784
  2478.6 119.2 %all-reduce.16 = (f32[4,768]{1,0:T(4,128)S(1)}, f32[768,16]{0,1:T(8,128)S(1)}) all-reduce(f32[4,768]{1,0:T(4,128)S(1)} %pad_maximum_fusion.1, f32[768,16]{0,1:T(8,128)S(1)} %fusion.186), channel_id=1, replica_groups=mesh['dp'=8,'tensor'=4] {'dp','tensor'}, use_global_device_ids=true, to_apply=%region_32.33 | all-reduce | flops 15360 | bytes 122880 | tf_op jit(solution)/shard_map/psum | solution.py:328
  2608.6 12.6 copy.276
  (421 shorter events, 448.3 us)
Async XLA Ops:
  7.2 97.0 %copy-start.42 = (bf16[192,96]{1,0:T(8,128)(2,1)S(1)}, bf16[192,96]{1,0:T(8,128)(2,1)}, u32[]{:S(2)}) copy-start(bf16[192,96]{1,0:T(8,128)(2,1)} %param.31) | copy-start | bytes 110596
  7.2 97.1 %copy-start.17 = (bf16[16,768,96]{1,2,0:T(8,128)(2,1)S(1)}, bf16[16,768,96]{1,2,0:T(8,128)(2,1)}, u32[]{:S(2)}) copy-start(bf16[16,768,96]{1,2,0:T(8,128)(2,1)} %param.34) | copy-start | bytes 7077892
  11.2 137.0 %all-to-all-start.1 = ((bf16[8,2,96,768]{3,2,1,0:T(8,128)(2,1)}), bf16[8,2,96,768]{3,2,1,0:T(8,128)(2,1)}, u32[]{:S(2)}, u32[]{:S(2)}) async-start(bf16[8,2,96,768]{3,2,1,0:T(8,128)(2,1)} %bitcast.13), calls=%async_computation.1 | async-start | bytes 4718592 | tf_op jit(solution)/shard_map/all_to_all | solution.py:196
  18.5 119.1 %all-gather.9.cloned.1.call-start = ((), (), s32[]{:S(2)}) async-start(), calls=%async_computation.17 | async-start | bytes 1536000 | tf_op jit(solution)/shard_map/all_gather | solution.py:75
  18.7 85.7 %copy-start.64 = (f32[197]{0:T(256)}, f32[197]{0:T(256)S(1)}, u32[]{:S(2)}) copy-start(f32[197]{0:T(256)S(1)} %broadcast_multiply_fusion.6) | copy-start | bytes 2368
  18.9 85.4 %copy-start.71 = (f32[197]{0:T(256)}, f32[197]{0:T(256)S(1)}, u32[]{:S(2)}) copy-start(f32[197]{0:T(256)S(1)} %add_rsqrt_fusion.1) | copy-start | bytes 2368
  19.0 85.4 %copy-start.52 = (f32[768]{0:T(1024)}, f32[768]{0:T(1024)S(1)}, u32[]{:S(2)}) copy-start(f32[768]{0:T(1024)S(1)} %get-tuple-element.135) | copy-start | bytes 9220
  19.0 165.2 %copy-start.54 = (f32[768]{0:T(1024)}, f32[768]{0:T(1024)S(1)}, u32[]{:S(2)}) copy-start(f32[768]{0:T(1024)S(1)} %get-tuple-element.136) | copy-start | bytes 9220
  19.0 165.2 %copy-start.73 = (f32[768]{0:T(1024)}, f32[768]{0:T(1024)S(1)}, u32[]{:S(2)}) copy-start(f32[768]{0:T(1024)S(1)} %get-tuple-element.98) | copy-start | bytes 9220
  148.2 84.8 %all-to-all-start.2 = ((bf16[8,2,96,768]{3,2,1,0:T(8,128)(2,1)}), bf16[8,2,96,768]{3,2,1,0:T(8,128)(2,1)}, u32[]{:S(2)}, u32[]{:S(2)}) async-start(bf16[8,2,96,768]{3,2,1,0:T(8,128)(2,1)} %bitcast.274), calls=%async_computation.2 | async-start | bytes 4718592 | tf_op jit(solution)/shard_map/all_to_all | solution.py:197
  152.6 55.1 %all-gather.11.cloned.1.call-start = ((), (), s32[]{:S(2)}) async-start(), calls=%async_computation.18 | async-start | bytes 1536000 | tf_op jit(solution)/shard_map/all_gather | solution.py:75
  179.0 2.5 collective-permute-start
  233.0 86.7 %all-to-all-start = ((bf16[8,2,147,768]{3,1,2,0:T(2,128)(2,1)}), bf16[8,2,147,768]{3,1,2,0:T(2,128)(2,1)}, u32[]{:S(2)}, u32[]{:S(2)}) async-start(bf16[8,2,147,768]{3,1,2,0:T(2,128)(2,1)} %copy.237), calls=%async_computation | async-start | bytes 7225344 | tf_op jit(solution)/shard_map/all_to_all | solution.py:195
  238.5 20.6 all-gather.13.cloned.1.call-start
  319.8 85.2 %all-to-all-start.4 = ((bf16[8,2,147,768]{3,1,2,0:T(2,128)(2,1)}), bf16[8,2,147,768]{3,1,2,0:T(2,128)(2,1)}, u32[]{:S(2)}, u32[]{:S(2)}) async-start(bf16[8,2,147,768]{3,1,2,0:T(2,128)(2,1)} %copy.245), calls=%async_computation.4 | async-start | bytes 7225344 | tf_op jit(solution)/shard_map/all_to_all | solution.py:230
  405.0 162.2 %all-to-all-start.3 = ((f32[2,1176,768]{2,0,1:T(2,128)}), f32[2,1176,768]{2,0,1:T(2,128)}, u32[]{:S(2)}, u32[]{:S(2)}) async-start(f32[2,1176,768]{2,0,1:T(2,128)} %copy.241), calls=%async_computation.3 | async-start | bytes 14450688 | tf_op jit(solution)/shard_map/all_to_all | solution.py:205
  567.2 162.1 %all-to-all-start.5 = ((f32[2,1176,768]{2,0,1:T(2,128)}), f32[2,1176,768]{2,0,1:T(2,128)}, u32[]{:S(2)}, u32[]{:S(2)}) async-start(f32[2,1176,768]{2,0,1:T(2,128)} %copy.247), calls=%async_computation.5 | async-start | bytes 14450688 | tf_op jit(solution)/shard_map/all_to_all | solution.py:245
  729.3 116.0 %all-to-all-start.7 = ((f32[2,768,768]{2,0,1:T(2,128)}), f32[2,768,768]{2,0,1:T(2,128)}, u32[]{:S(2)}, u32[]{:S(2)}) async-start(f32[2,768,768]{2,0,1:T(2,128)} %copy.269), calls=%async_computation.7 | async-start | bytes 9437184 | tf_op jit(solution)/shard_map/all_to_all | solution.py:247
  822.8 20.5 collective-permute-start.2
  838.6 17.6 collective-permute-start.1
  845.3 116.5 %all-to-all-start.6 = ((f32[2,768,768]{2,0,1:T(2,128)}), f32[2,768,768]{2,0,1:T(2,128)}, u32[]{:S(2)}, u32[]{:S(2)}) async-start(f32[2,768,768]{2,0,1:T(2,128)} %copy.267), calls=%async_computation.6 | async-start | bytes 9437184 | tf_op jit(solution)/shard_map/all_to_all | solution.py:246
  851.3 32.0 %all-gather.15.cloned.1.call-start = ((), (), s32[]{:S(2)}) async-start(), calls=%async_computation.20 | async-start | bytes 1536000 | tf_op jit(solution)/shard_map/all_gather | solution.py:75
  864.9 127.9 %reduce-scatter.19.cloned.1.call-start = ((), (), s32[]{:S(2)}) async-start(), calls=%async_computation.22 | async-start | bytes 884736
  900.8 161.6 %reduce-scatter.17.cloned.1.call-start = ((), (), s32[]{:S(2)}) async-start(), calls=%async_computation.21 | async-start | bytes 2211840
  917.7 575.7 %all-reduce.25.cloned.1.call-start = ((), (), s32[]{:S(2)}) async-start(), calls=%async_computation.12 | async-start | bytes 11796480 | tf_op jit(solution)/shard_map/psum | solution.py:83
  993.8 69.7 %copy-start.38 = (f32[192,96]{1,0:T(8,128)}, f32[192,96]{1,0:T(8,128)S(1)}, u32[]{:S(2)}) copy-start(f32[192,96]{1,0:T(8,128)S(1)} %multiply_add_fusion.5) | copy-start | bytes 221188
  1381.1 349.2 %all-reduce.27.cloned.1.call-start = ((), (), s32[]{:S(2)}) async-start(), calls=%async_computation.13 | async-start | bytes 11796480 | tf_op jit(solution)/shard_map/psum | solution.py:83
  1616.8 306.3 %all-reduce.29.cloned.1.call-start = ((), (), s32[]{:S(2)}) async-start(), calls=%async_computation.14 | async-start | bytes 11796480 | tf_op jit(solution)/shard_map/psum | solution.py:83
  1809.6 306.7 %all-reduce.31.cloned.1.call-start = ((), (), s32[]{:S(2)}) async-start(), calls=%async_computation.15 | async-start | bytes 11796480 | tf_op jit(solution)/shard_map/psum | solution.py:83
  2002.7 306.2 %all-reduce.33.cloned.1.call-start = ((), (), s32[]{:S(2)}) async-start(), calls=%async_computation.16 | async-start | bytes 11796480 | tf_op jit(solution)/shard_map/psum | solution.py:83
  2366.1 242.5 %all-to-all-start.9 = ((bf16[1,5,768,768]{3,1,0,2:T(8,128)(2,1)}), bf16[1,5,768,768]{3,1,0,2:T(8,128)(2,1)}, u32[]{:S(2)}, u32[]{:S(2)}) async-start(bf16[1,5,768,768]{3,1,0,2:T(8,128)(2,1)} %copy.275), calls=%async_computation.9 | async-start | bytes 18874368 | tf_op jit(solution)/shard_map/all_to_all | solution.py:373
  2418.3 52.4 %copy-start.8 = (f32[197,768]{1,0:T(8,128)S(1)}, f32[197,768]{1,0:T(8,128)}, u32[]{:S(2)}) copy-start(f32[197,768]{1,0:T(8,128)} %copy-done.6) | copy-start | bytes 1815556
  2418.3 52.4 %copy-start.56 = (f32[768]{0:T(1024)S(1)}, f32[768]{0:T(1024)}, u32[]{:S(2)}) copy-start(f32[768]{0:T(1024)} %copy-done.54) | copy-start | bytes 9220
  2418.4 52.4 %copy-start.60 = (bf16[197,16]{0,1:T(8,128)(2,1)S(1)}, bf16[197,16]{0,1:T(8,128)(2,1)}, u32[]{:S(2)}) copy-start(bf16[197,16]{0,1:T(8,128)(2,1)} %multiply_convert_fusion.2) | copy-start | bytes 18916
  2418.4 52.4 %copy-start.63 = (f32[197]{0:T(256)S(1)}, f32[197]{0:T(256)}, u32[]{:S(2)}) copy-start(f32[197]{0:T(256)} %copy-done.61) | copy-start | bytes 2368
  2418.4 52.7 %copy-start.76 = (f32[768]{0:T(1024)S(1)}, f32[768]{0:T(1024)}, u32[]{:S(2)}) copy-start(f32[768]{0:T(1024)} %get-tuple-element.93) | copy-start | bytes 9220
  2418.4 52.7 %copy-start.75 = (f32[768]{0:T(1024)S(1)}, f32[768]{0:T(1024)}, u32[]{:S(2)}) copy-start(f32[768]{0:T(1024)} %get-tuple-element.86) | copy-start | bytes 9220
  2418.4 59.6 %copy-start.13 = (bf16[197,768]{1,0:T(8,128)(2,1)S(1)}, bf16[197,768]{1,0:T(8,128)(2,1)}, u32[]{:S(2)}) copy-start(bf16[197,768]{1,0:T(8,128)(2,1)} %param.24) | copy-start | bytes 907780
  2418.4 59.6 %copy-start.53 = (f32[768]{0:T(1024)S(1)}, f32[768]{0:T(1024)}, u32[]{:S(2)}) copy-start(f32[768]{0:T(1024)} %copy-done.52) | copy-start | bytes 9220
  2418.4 59.6 %copy-start.65 = (f32[197]{0:T(256)S(1)}, f32[197]{0:T(256)}, u32[]{:S(2)}) copy-start(f32[197]{0:T(256)} %copy-done.64) | copy-start | bytes 2368
  2418.5 59.6 %copy-start.72 = (f32[197]{0:T(256)S(1)}, f32[197]{0:T(256)}, u32[]{:S(2)}) copy-start(f32[197]{0:T(256)} %copy-done.71) | copy-start | bytes 2368
  2418.5 179.3 %copy-start.59 = (f32[768,16]{0,1:T(8,128)S(1)}, f32[768,16]{0,1:T(8,128)}, u32[]{:S(2)}) copy-start(f32[768,16]{0,1:T(8,128)} %param.37) | copy-start | bytes 147460
  2422.7 181.0 %copy-start.67 = (f32[2,768]{1,0:T(2,128)S(1)}, f32[2,768]{1,0:T(2,128)}, u32[]{:S(2)}) copy-start(f32[2,768]{1,0:T(2,128)} %param.28) | copy-start | bytes 18436
  2422.7 182.3 %copy-start.41 = (bf16[768,16]{0,1:T(8,128)(2,1)S(1)}, bf16[768,16]{0,1:T(8,128)(2,1)}, u32[]{:S(2)}) copy-start(bf16[768,16]{0,1:T(8,128)(2,1)} %param.32) | copy-start | bytes 73732
  2468.6 138.0 %copy-start.33 = (f32[197,768]{1,0:T(8,128)S(1)}, f32[197,768]{1,0:T(8,128)}, u32[]{:S(2)}) copy-start(f32[197,768]{1,0:T(8,128)} %get-tuple-element.117) | copy-start | bytes 1815556
  2468.6 139.1 %copy-start.32 = (f32[3,96,192]{1,2,0:T(8,128)S(1)}, f32[3,96,192]{1,2,0:T(8,128)}, u32[]{:S(2)}) copy-start(f32[3,96,192]{1,2,0:T(8,128)} %copy-done.31) | copy-start | bytes 663556
  2469.5 6.5 collective-permute-start.4
  2471.9 127.2 %collective-permute-start.3 = (f32[9,768]{1,0:T(8,128)S(1)}, f32[9,768]{1,0:T(8,128)S(1)}, u32[]{:S(2)}, u32[]{:S(2)}) collective-permute-start(f32[9,768]{1,0:T(8,128)S(1)} %slice.101), channel_id=1, source_target_pairs={{0,1},{1,2},{2,3},{4,5},{5,6},{6,7},{8,9},{9,10},{10,11},{12,13},{... | collective-permute-start | bytes 82952
  (63 other events, 893.8 us)
Sparse Core Ops, SparseCore 0:
  21.4 19.1 all-gather.8
  185.7 21.8 all-gather.10
  240.9 18.1 all-gather.12
  865.0 18.1 all-gather.14
  900.9 91.8 reduce-scatter.18
  996.5 65.8 reduce-scatter.16
  1381.2 112.1 all-reduce.24
  1616.9 113.3 all-reduce.26
  1809.7 113.3 all-reduce.28
  2002.8 113.3 all-reduce.30
  2195.5 113.3 all-reduce.32
where the time goes:
time: 2670 us; the launch traced here: 2660 us
  waiting for transfers between devices  1070 us (40%)
  blocking collectives  589 us (22%)
  matrix products  472 us (18%)
  local copies, waits for them, and re-layouts  350 us (13%)
  other arithmetic  95.3 us (4%)
  starting transfers between devices  62.8 us (2%)
    psum x5, waiting for transfers between devices, gram(): lax.psum(jnp.einsum('kic,kjc->kij', blocks, blocks, precision=HIGH).astyp...  566 us
    all_to_all x1, blocking collectives, local(): lax.all_to_all(outgoing, 'dp', split_axis=0, concat_axis=2, tiled=True)[0]  259 us
    dot_general x5, matrix products, local(): jnp.einsum('kij,kjc->kic', poly_term, orthogonal, precision=HIGH)  175 us
    dot_general x5, matrix products, gram(): jnp.einsum('kic,kjc->kij', blocks, blocks, precision=HIGH)  157 us
    all_to_all x1, waiting for transfers between devices, local(): lax.all_to_all(host_row_grad, 'dp', split_axis=1, concat_axis=0, tiled=True)  145 us
    all_to_all x1, waiting for transfers between devices, local(): lax.all_to_all(host_out, 'dp', split_axis=1, concat_axis=0, tiled=True)  137 us
    psum x1, blocking collectives, local(): vec_grad, router_grad = lax.psum((vec_part, router_part), ('dp', 'tensor'))  119 us
    unnamed x3, blocking collectives  100 us
  transfers between devices with their start and end apart: 25, of which 15 were waited for; matrix products, arithmetic and copies ran while one was open for 18% of the time, Pallas kernels for 0%

commit v1 on v0

v1 whole, which is shorter than its diff:
```python
import math

import jax
import jax.numpy as jnp
from jax import lax
from jax.experimental import pallas as pl
from jax.experimental.pallas import tpu as pltpu
from jax.sharding import PartitionSpec as P

D = 768
HD = 64
FF = 3072
CAP = 147
EXPERTS = 16
SEQ = 197

HIGH = lax.Precision.HIGHEST
LN_EPS = 1e-06
NS_EPS = 1e-07
NS_A = 3.4445
NS_B = -4.775
NS_C = 2.0315
DECAY = 0.5
VEC_RATE = 0.0002
INV_ROOT_TWO = 0.7071067811865476
INV_ROOT_TWO_PI = 0.3989422804014327
BF = jnp.bfloat16
F32 = jnp.float32


def mm(spec, left, right):
    return jnp.einsum(spec, left, right, preferred_element_type=F32)


def after(value, other):
    return lax.optimization_barrier((value, other))[0]


def apply_layer_norm(values, gain_row, offset_row):
    centre = values - jnp.mean(values, axis=-1, keepdims=True)
    inv_std = lax.rsqrt(jnp.mean(centre * centre, axis=-1, keepdims=True) + LN_EPS)
    normed = centre * inv_std
    return (normed * gain_row + offset_row, normed, inv_std)


def norm_back(grad_normed, normed, inv_std, gain_row):
    scaled = grad_normed * gain_row
    first_mean = jnp.mean(scaled, axis=-1, keepdims=True)
    second_mean = jnp.mean(scaled * normed, axis=-1, keepdims=True)
    grad_values = inv_std * (scaled - first_mean - normed * second_mean)
    gain_grad = jnp.sum(grad_normed * normed, axis=0, keepdims=True)
    return (grad_values, gain_grad, jnp.sum(grad_normed, axis=0, keepdims=True))


def local_orthogonalize(matrix):
    norm_value = jnp.sqrt(jnp.sum(matrix * matrix))
    current = matrix / (norm_value + NS_EPS)
    for repeat in range(5):
        square = jnp.dot(current, current.T, precision=HIGH)
        poly_term = NS_B * square + NS_C * jnp.dot(square, square, precision=HIGH)
        current = NS_A * current + jnp.dot(poly_term, current, precision=HIGH)
    return current


def orthogonalize(matrix):
    wide = matrix.astype(F32)
    inverse = 1.0 / (jnp.sqrt(jnp.sum(wide * wide)) + NS_EPS)
    rows = matrix.shape[0]
    unit = (
        lax.broadcasted_iota(jnp.int32, (rows, rows), 0)
        == lax.broadcasted_iota(jnp.int32, (rows, rows), 1)
    ).astype(F32)
    current = matrix
    for repeat in range(5):
        square = mm("ic,jc->ij", current, current)
        if repeat == 0:
            square = square * (inverse * inverse)
        rest = (square - unit).astype(BF)
        poly = (
            (NS_A - NS_C) * unit + (NS_B + 2.0 * NS_C) * square + NS_C * mm("ij,jk->ik", rest, rest)
        ).astype(BF)
        grown = mm("ij,jc->ic", poly, current)
        if repeat == 0:
            grown = grown * inverse
        current = grown.astype(BF)
    return current


def dot(left, right, left_dim, right_dim):
    return lax.dot_general(
        left, right, (((left_dim,), (right_dim,)), ((), ())), preferred_element_type=F32
    )


class Ortho:
    def __init__(self, current, square, rest, poly, size):
        self.current, self.square, self.rest, self.poly, self.size = (
            current, square, rest, poly, size
        )
        self.n = square.shape[0]
        self.blocks, self.w = current.shape[0], current.shape[-1]
        self.tile = 256
        self.cuts = [(i, i + self.tile) for i in range(0, self.n, self.tile)]

    def unit(self, first, last):
        shape = (last - first, self.n - first)
        return (
            lax.broadcasted_iota(jnp.int32, shape, 0) == lax.broadcasted_iota(jnp.int32, shape, 1)
        ).astype(F32)

    def clear(self):
        self.square[...] = jnp.zeros_like(self.square)

    def add_square(self, b):
        block = self.current[b].reshape(self.n, self.w)
        for first, last in self.cuts:
            self.square[first:last, first:] += dot(block[first:last, :], block[first:, :], 1, 1)

    def make_poly(self):
        square, rest, poly, cuts = self.square, self.rest, self.poly, self.cuts
        scale = self.size[...]
        scale_two = scale * scale
        for first, last in cuts:
            for low, high in cuts:
                if low > first:
                    square[low:high, first:last] = square[first:last, low:high].T
        for first, last in cuts:
            if first > 0:
                rest[first:last, :first] = (square[first:last, :first] * scale_two).astype(BF)
            rest[first:last, first:] = (
                square[first:last, first:] * scale_two - self.unit(first, last)
            ).astype(BF)
        for first, last in cuts:
            strip = scale * (
                (NS_A - NS_C) * self.unit(first, last)
                + (NS_B + 2.0 * NS_C) * scale_two * square[first:last, first:]
                + NS_C * dot(rest[first:last, :], rest[:, first:], 1, 0)
            )
            poly[first:last, first:] = strip.astype(BF)
            for low, high in cuts:
                if low > first:
                    poly[low:high, first:last] = strip[:, low - first : high - first].T.astype(BF)

    def measure(self):
        total = jnp.zeros((1, 1), F32)
        for first, last in self.cuts:
            diagonal = self.unit(first, last)[:, : self.tile] * self.square[first:last, first:last]
            total = total + jnp.sum(
                jnp.sum(diagonal, axis=1, keepdims=True), axis=0, keepdims=True
            )
        self.size[...] = 1.0 / (jnp.sqrt(total) + NS_EPS)

    def grown(self, b):
        block = self.current[b].reshape(self.n, self.w)
        return dot(self.poly[...], block, 1, 0).astype(BF)

    def steps(self):
        self.measure()

        @pl.loop(0, 4)
        def _(step):
            self.make_poly()
            self.size[...] = jnp.ones((1, 1), F32)
            self.clear()

            @pl.loop(0, self.blocks)
            def _(b):
                self.current[b] = self.grown(b).reshape(self.current.shape[1:])
                self.add_square(b)

        self.make_poly()


def ortho_kernel(x_ref, current, poly, square, rest, size):
    ortho = Ortho(current, square, rest, poly, size)
    ortho.clear()

    @pl.loop(0, ortho.blocks)
    def _(b):
        current[b] = x_ref[b]
        ortho.add_square(b)

    ortho.steps()


def ortho_call(blocks):
    count, n, w = blocks.shape
    vmem = pl.BlockSpec(memory_space=pltpu.VMEM)
    return pl.pallas_call(
        ortho_kernel,
        out_shape=(jax.ShapeDtypeStruct((count, n, w), BF), jax.ShapeDtypeStruct((n, n), BF)),
        in_specs=[vmem],
        out_specs=(vmem, vmem),
        scratch_shapes=[
            pltpu.VMEM((n, n), F32), pltpu.VMEM((n, n), BF), pltpu.VMEM((1, 1), F32)
        ],
        cost_estimate=pl.CostEstimate(
            flops=20 * count * n * n * w, bytes_accessed=4 * count * n * w, transcendentals=0
        ),
        compiler_params=pltpu.CompilerParams(vmem_limit_bytes=50 * 1024 * 1024),
        name="orthogonalize",
    )(blocks)


MESH = pl.DeviceIdType.MESH
PEERS = (4, 1, 5, 2, 6, 3, 7)


def experts_kernel(
    slots_ref, win_ref, wexp_ref,
    came_ref, gin_ref, gexp_ref,
    rows, weights, part, other, rows_of, hidden_of,
    tok_send, tok_recv, fwd_send, fwd_recv, sum_send, sum_recv, ret_send, ret_recv,
    wx_send, wx_recv, load_sem,
):
    n_experts, n_t, n_dp, pair, width = rows.shape
    quarter = pair // 2
    share = gin_ref.shape[2]
    d, t = lax.axis_index("dp"), lax.axis_index("tensor")
    sibling, across = (d, t ^ 1), (d, t ^ 2)
    count = n_dp * quarter

    def remote(source, target, send, recv, device):
        return pltpu.make_async_remote_copy(
            src_ref=source, dst_ref=target, send_sem=send, recv_sem=recv,
            device_id=device, device_id_type=MESH,
        )

    def tok(e, k):
        return remote(
            slots_ref.at[d ^ k, e], rows.at[e, 0, k],
            tok_send.at[e, k], tok_recv.at[e, k], (d ^ k, t),
        )

    def tok_own(e):
        return pltpu.make_async_copy(slots_ref.at[d, e], rows.at[e, 0, 0], tok_recv.at[e, 0])

    def forward(kind, e, k):
        source, target = ((0, 1), (0, 2), (2, 3))[kind]
        return remote(
            rows.at[e, source, k], rows.at[e, target, k],
            fwd_send.at[kind, e, k], fwd_recv.at[kind, e, k],
            across if kind == 1 else sibling,
        )

    def partial(stage, e):
        return remote(
            part.at[e, 3 - stage], other.at[e, stage],
            sum_send.at[stage, e], sum_recv.at[stage, e],
            across if stage == 1 else sibling,
        )

    def ret(e, k):
        return remote(
            part.at[e, 0, k], came_ref.at[d, e],
            ret_send.at[e, k], ret_recv.at[e, k], (d ^ k, t),
        )

    def ret_own(e):
        return pltpu.make_async_copy(part.at[e, 0, 0], came_ref.at[d, e], ret_recv.at[e, 0])

    def load(e):
        return pltpu.make_async_copy(win_ref.at[:, e], weights.at[0, e], load_sem.at[e])

    def second(e, k):
        return remote(
            wexp_ref.at[d ^ k, e], weights.at[1, e, d], wx_send.at[e, k], wx_recv.at[e, k], (d ^ k, t)
        )

    def second_own(e):
        return pltpu.make_async_copy(wexp_ref.at[d, e], weights.at[1, e, d], wx_recv.at[e, 0])

    def send(e):
        for k in PEERS:
            tok(e, k).start()
        for k in PEERS:
            second(e, k).start()

    def wait_second(e):
        second_own(e).wait()

        @pl.loop(1, n_dp)
        def _(k):
            second(e, k).wait_recv()

    barrier = pltpu.get_barrier_semaphore()

    @pl.loop(1, n_dp)
    def _(k):
        pl.semaphore_signal(barrier, inc=1, device_id=(d ^ k, t), device_id_type=MESH)

    pl.semaphore_signal(barrier, inc=1, device_id=sibling, device_id_type=MESH)
    pl.semaphore_signal(barrier, inc=1, device_id=across, device_id_type=MESH)
    for e in range(n_experts):
        tok_own(e).start()
        load(e).start()
        second_own(e).start()
    pl.semaphore_wait(barrier, n_dp + 1)
    send(0)

    def pass_on(e):
        for k in (0,) + PEERS:
            if k == 0:
                tok_own(e).wait()
            else:
                tok(e, k).wait_recv()
            forward(0, e, k).start()
            forward(1, e, k).start()

    def pass_again(e):
        for k in (0,) + PEERS:
            forward(1, e, k).wait_recv()
            forward(2, e, k).start()

        @pl.loop(0, n_dp)
        def _(k):
            forward(0, e, k).wait_recv()
            forward(2, e, k).wait_recv()

    def give_back(e):
        partial(1, e).wait_recv()
        partial(2, e).wait_recv()
        for k in range(n_dp):
            part[e, 0, k] = (
                part[e, 0, k].astype(F32) + other[e, 1, k].astype(F32) + other[e, 2, k].astype(F32)
            ).astype(BF)
        ret_own(e).start()
        for k in PEERS:
            ret(e, k).start()

    def weight_grads(e):
        gin_ref[:, e] = dot(rows_of[0], hidden_of[1], 0, 0).astype(BF).reshape(n_dp, share, width)
        gexp_ref[:, e] = dot(rows_of[1], hidden_of[0], 0, 0).astype(BF).reshape(n_dp, share, width)

    pass_on(0)
    send(1)
    pass_again(0)
    wait_second(0)
    for e in range(n_experts):
        load(e).wait()

    @pl.loop(0, n_experts * n_t)
    def _(step):
        e = step // n_t
        r = n_t - 1 - step % n_t
        w_in = weights[0, e].reshape(width, width)
        w_exp = weights[1, e].reshape(width, width)
        pairs = [rows[e, r, k].astype(F32) for k in range(n_dp)]
        act_rows = jnp.concatenate([block[:quarter] for block in pairs], axis=0).astype(BF)
        grad_rows = jnp.concatenate([block[quarter:] for block in pairs], axis=0).astype(BF)
        pre = dot(act_rows, w_in, 1, 0)
        normal = 0.5 * (1.0 + lax.erf(pre * INV_ROOT_TWO))
        slope = normal + pre * jnp.exp(-0.5 * pre * pre) * INV_ROOT_TWO_PI
        act = (pre * normal).astype(BF)
        grad_pre = (dot(grad_rows, w_exp, 1, 0) * slope).astype(BF)
        at = pl.ds(pl.multiple_of(r * count, count), count)
        rows_of[0, at] = act_rows
        rows_of[1, at] = grad_rows
        hidden_of[0, at] = act
        hidden_of[1, at] = grad_pre
        row_out, row_grad = dot(act, w_exp, 1, 1), dot(grad_pre, w_in, 1, 1)
        for k in range(n_dp):
            own = slice(k * quarter, (k + 1) * quarter)
            part[e, r, k] = jnp.concatenate([row_out[own], row_grad[own]], axis=0).astype(BF)

        @pl.when(r == n_t - 1)
        def _():
            partial(0, e).start()

        @pl.when(r == 2)
        def _():
            partial(0, e).wait_recv()
            for k in range(n_dp):
                part[e, 2, k] = (
                    part[e, 2, k].astype(F32) + other[e, 0, k].astype(F32)
                ).astype(BF)
            partial(1, e).start()

        @pl.when(r == 1)
        def _():
            partial(2, e).start()

        @pl.when(step == n_t - 1)
        def _():
            pass_on(1)
            weight_grads(0)
            give_back(0)
            pass_again(1)
            wait_second(1)

        @pl.when(step == 2 * n_t - 1)
        def _():
            weight_grads(1)
            give_back(1)

    for e in range(n_experts):
        ret_own(e).wait()
        for stage in range(3):
            partial(stage, e).wait_send()

        @pl.loop(0, n_dp)
        def _(k, e=e):
            for kind in range(3):
                forward(kind, e, k).wait_send()

        @pl.loop(1, n_dp)
        def _(k, e=e):
            tok(e, k).wait_send()
            second(e, k).wait_send()
            ret(e, k).wait_send()
            ret(e, k).wait_recv()


def experts_call(slots, w_in, w_exp):
    n_dp, n_experts, pair, width = slots.shape
    share = w_in.shape[2]
    n_t = lax.axis_size("tensor")
    anywhere = pl.BlockSpec(memory_space=pl.ANY)
    vmem = pl.BlockSpec(memory_space=pltpu.VMEM)
    grads = jax.ShapeDtypeStruct((n_dp, n_experts, share, width), BF)
    dma = pltpu.SemaphoreType.DMA
    part = (n_experts, n_t, n_dp, pair, width)
    rows = n_experts * n_t * n_dp * pair
    return pl.pallas_call(
        experts_kernel,
        out_shape=(jax.ShapeDtypeStruct(slots.shape, BF), grads, grads),
        in_specs=[anywhere] * 3,
        out_specs=(anywhere, vmem, vmem),
        scratch_shapes=[
            pltpu.VMEM(part, BF),
            pltpu.VMEM((2, n_experts, n_dp, share, width), BF),
            pltpu.VMEM(part, BF),
            pltpu.VMEM((n_experts, 3) + part[2:], BF),
            pltpu.VMEM((2, n_t * n_dp * pair // 2, width), BF),
            pltpu.VMEM((2, n_t * n_dp * pair // 2, width), BF),
            dma((n_experts, n_dp)),
            dma((n_experts, n_dp)),
            dma((3, n_experts, n_dp)),
            dma((3, n_experts, n_dp)),
            dma((3, n_experts)),
            dma((3, n_experts)),
            dma((n_experts, n_dp)),
            dma((n_experts, n_dp)),
            dma((n_experts, n_dp)),
            dma((n_experts, n_dp)),
            dma((n_experts,)),
        ],
        cost_estimate=pl.CostEstimate(
            flops=40 * rows * width * width, bytes_accessed=400_000_000, transcendentals=0
        ),
        compiler_params=pltpu.CompilerParams(
            collective_id=1, has_side_effects=True, vmem_limit_bytes=60 * 1024 * 1024
        ),
        name="experts",
    )(slots, w_in, w_exp)


def layer_norm_parts(values):
    centre = values - jnp.mean(values, axis=-1, keepdims=True)
    inv_std = lax.rsqrt(jnp.mean(centre * centre, axis=-1, keepdims=True) + LN_EPS)
    return centre * inv_std, inv_std


def remote(source, target, send, recv, device):
    return pltpu.make_async_remote_copy(
        src_ref=source, dst_ref=target, send_sem=send, recv_sem=recv,
        device_id=device, device_id_type=MESH,
    )


def greet(n_dp, d, t, more=0):
    barrier = pltpu.get_barrier_semaphore()

    @pl.loop(1, n_dp)
    def _(k):
        pl.semaphore_signal(barrier, inc=1, device_id=(d ^ k, t), device_id_type=MESH)

    pl.semaphore_signal(barrier, inc=1, device_id=(d, t ^ 1), device_id_type=MESH)
    pl.semaphore_signal(barrier, inc=1, device_id=(d, t ^ 2), device_id_type=MESH)
    pl.semaphore_wait(barrier, n_dp + 1 + more)


class Gather:
    def __init__(self, blocks, send, recv, d, t):
        self.copies = [
            remote(blocks.at[i], blocks.at[i], send.at[n], recv.at[n], (d, t ^ hop))
            for n, (i, hop) in enumerate(((t, 1), (t, 2), (t ^ 2, 1)))
        ]

    def start(self):
        self.copies[0].start()
        self.copies[1].start()

    def pass_on(self):
        self.copies[1].wait_recv()
        self.copies[2].start()

    def finish(self):
        self.copies[0].wait_recv()
        self.copies[2].wait_recv()

    def wait_sent(self):
        for copy in self.copies:
            copy.wait_send()


class Scatter:
    def __init__(self, block, landed, send, recv, d, t):
        self.block, self.landed = block, landed
        self.copies = [
            remote(block(3 - n), landed.at[n], send.at[n], recv.at[n], (d, t ^ hop))
            for n, hop in enumerate((1, 2, 1))
        ]

    def send(self, r):
        if r == 2:
            self.copies[0].wait_recv()
            own = self.block(2)
            own[...] = (own[...].astype(F32) + self.landed[0].astype(F32)).astype(BF)
        self.copies[3 - r].start()

    def total(self):
        self.copies[1].wait_recv()
        self.copies[2].wait_recv()
        return (
            self.block(0)[...].astype(F32)
            + self.landed[1].astype(F32)
            + self.landed[2].astype(F32)
        )

    def wait_sent(self):
        for copy in self.copies:
            copy.wait_send()


class Exchange:
    def __init__(self, blocks, target, send, recv, d, t):
        self.n_dp = blocks.shape[0]
        self.parts = (blocks, target, send, recv, d, t)

    def copy(self, k):
        blocks, target, send, recv, d, t = self.parts
        return remote(blocks.at[d ^ k], target.at[d], send.at[k], recv.at[k], (d ^ k, t))

    def own(self):
        blocks, target, send, recv, d, t = self.parts
        return pltpu.make_async_copy(blocks.at[d], target.at[d], recv.at[0])

    def start(self):
        self.own().start()
        for k in PEERS:
            self.copy(k).start()

    def finish(self):
        self.own().wait()

        @pl.loop(1, self.n_dp)
        def _(k):
            self.copy(k).wait_recv()

    def wait_sent(self):
        @pl.loop(1, self.n_dp)
        def _(k):
            self.copy(k).wait_send()


class Spread:
    def __init__(self, source, blocks, send, recv, d, t):
        self.own = pltpu.make_async_copy(source, blocks.at[d], recv.at[0])
        self.first = [
            remote(source, blocks.at[d], send.at[k], recv.at[k], (d ^ k, t)) for k in (1, 2, 4, 6)
        ]
        self.onward = [
            remote(blocks.at[d ^ k], blocks.at[d ^ k], send.at[k ^ 1], recv.at[k ^ 1], (d ^ 1, t))
            for k in (2, 4, 6)
        ]

    def start(self):
        self.own.start()
        for copy in (self.first[2], self.first[3], self.first[1], self.first[0]):
            copy.start()

    def finish(self):
        for n in range(3):
            self.first[n + 1].wait_recv()
            self.onward[n].start()
        self.own.wait()
        self.first[0].wait_recv()
        for copy in self.onward:
            copy.wait_recv()

    def wait_sent(self):
        for copy in self.first + self.onward:
            copy.wait_send()


def of_head(block, head):
    lane = lax.broadcasted_iota(jnp.int32, block.shape, 1)
    return jnp.where(lane // HD == head, block, jnp.zeros_like(block))


def head_probs(query, key, head):
    scores = dot(of_head(query, head), key, 1, 1) * HD ** (-0.5)
    seen = lax.broadcasted_iota(jnp.int32, scores.shape, 1) < SEQ
    scores = jnp.where(seen, scores, -1e30)
    expo = jnp.exp(scores - jnp.max(scores, axis=-1, keepdims=True))
    return expo / jnp.sum(expo, axis=-1, keepdims=True)


def only_tokens(block):
    row = lax.broadcasted_iota(jnp.int32, block.shape, 0)
    return jnp.where(row < SEQ, block, jnp.zeros_like(block))


def front_kernel(
    local_heads,
    x_ref, cot_ref, wp_ref, gains_ref, biases_ref, ids_ref, wr_ref, win_ref,
    a1_out, three_out, mixed_out, w_out, slots_out, middle_ref, cots_ref, gate_ref, slot_ref, win_out,
    a1, cot, a2, three, mixed, w, part, landed, slots,
    wt_send, wt_recv, in_send, in_recv,
    ag_send, ag_recv, sum_send, sum_recv, out_sem,
):
    n_dp, share, wide = w.shape
    n_t, rows, width = a1.shape
    third = width // 3
    d, t = lax.axis_index("dp"), lax.axis_index("tensor")
    greet(n_dp, d, t)

    weights = Spread(wp_ref, w, wt_send, wt_recv, d, t)
    weights.start()
    gathers = [Gather(ref, ag_send.at[n], ag_recv.at[n], d, t) for n, ref in enumerate((a1, cot, a2))]
    x = x_ref[...].astype(F32)
    normed, _ = layer_norm_parts(x)
    a1[t] = only_tokens(normed * gains_ref[0:1, :] + biases_ref[0:1, :]).astype(BF)
    cot[t] = cot_ref[...]
    gathers[0].start()
    gathers[1].start()
    gathers[0].pass_on()
    gathers[0].finish()
    weights.finish()
    bulk_in = Exchange(win_ref, win_out, in_send, in_recv, d, t)
    bulk_in.start()

    experts, quarter = wr_ref.shape[0], slots.shape[2] // 2
    label = lax.broadcasted_iota(jnp.int32, (experts, rows), 0)
    earlier = (
        lax.broadcasted_iota(jnp.int32, (rows, rows), 0)
        < lax.broadcasted_iota(jnp.int32, (rows, rows), 1)
    ).astype(BF)
    taken = jnp.zeros((experts, 1), F32)
    first_place = (t * quarter).astype(F32)
    chosen = []
    for image in range(n_t):
        named = [label == ids_ref[image, k : k + 1, :] for k in range(2)]
        chosen.append(named)
        counted = named[0].astype(F32) + named[1].astype(F32)
        before = taken + dot(counted.astype(BF), earlier, 1, 0)
        taken = taken + jnp.sum(counted, axis=1, keepdims=True)
        for k in range(2):
            place = jnp.sum(jnp.where(named[k], before, 0.0), axis=0, keepdims=True) - first_place
            ids = ids_ref[image, k : k + 1, :].astype(F32)
            mine = (place >= 0.0) & (place < quarter) & (ids >= 0.0)
            slot_ref[image, k : k + 1, :] = jnp.where(mine, ids * quarter + place, -1.0)

    sums = Scatter(lambda r: part.at[r], landed, sum_send, sum_recv, d, t)
    for r in reversed(range(n_t)):
        image = t ^ r
        every = w[...].reshape(n_dp * share, wide)
        qkv = dot(a1[image], every[:, :width], 1, 0).astype(BF)
        three[image] = qkv
        query, key, value = [qkv[:, s * third : (s + 1) * third] for s in range(3)]
        heads = jnp.zeros((rows, third), F32)
        for head in range(local_heads):
            probs = head_probs(query, key, head).astype(BF)
            heads = heads + dot(probs, of_head(value, head), 1, 0)
        mixed[image] = heads.astype(BF)
        part[r] = dot(mixed[image], every[:, width:], 1, 1).astype(BF)
        if r > 0:
            sums.send(r)
        if r == 1:
            gathers[1].pass_on()
    middle = x + only_tokens(sums.total())
    middle_ref[...] = middle
    normed, _ = layer_norm_parts(middle)
    a2[t] = only_tokens(normed * gains_ref[1:2, :] + biases_ref[1:2, :]).astype(BF)
    gathers[2].start()
    outs = [
        pltpu.make_async_copy(source, target, out_sem.at[n])
        for n, (source, target) in enumerate(
            ((a1, a1_out), (three, three_out), (mixed, mixed_out), (w, w_out), (slots, slots_out))
        )
    ]
    for out in outs[:4]:
        out.start()
    gathers[1].finish()
    gathers[2].pass_on()
    gathers[2].finish()

    gates = []
    for image in range(n_t):
        logits = dot(wr_ref[...], a2[image], 1, 1)
        expo = jnp.exp(logits - jnp.max(logits, axis=0, keepdims=True))
        probs = expo / jnp.sum(expo, axis=0, keepdims=True)
        gates.append(
            [jnp.sum(jnp.where(chosen[image][k], probs, 0.0), axis=0, keepdims=True) for k in range(2)]
        )
    pairs = slots.shape[1]
    held = pairs * quarter

    @pl.loop(0, n_dp)
    def _(host):
        number = lax.broadcasted_iota(jnp.int32, (held, rows), 0) + host * held
        number = number.astype(F32)
        slot_act = jnp.zeros((held, width), F32)
        slot_cot = jnp.zeros((held, width), F32)
        gate = jnp.zeros((held, 1), F32)
        for image in range(n_t):
            picks = [slot_ref[image, k : k + 1, :] == number for k in range(2)]
            spread = jnp.where(picks[0] | picks[1], 1.0, 0.0).astype(BF)
            slot_act = slot_act + dot(spread, a2[image], 1, 0)
            slot_cot = slot_cot + dot(spread, cot[image], 1, 0)
            for k in range(2):
                gate = gate + jnp.sum(
                    jnp.where(picks[k], gates[image][k], 0.0), axis=1, keepdims=True
                )
        slot_grad = gate * slot_cot
        gate_ref[host] = gate
        cots_ref[host] = slot_cot.astype(BF)
        for e in range(pairs):
            own = slice(e * quarter, (e + 1) * quarter)
            slots[host, e] = jnp.concatenate([slot_act[own], slot_grad[own]], axis=0).astype(BF)

    outs[4].start()
    for out in outs:
        out.wait()
    weights.wait_sent()
    sums.wait_sent()
    for gather in gathers:
        gather.wait_sent()
    bulk_in.finish()
    bulk_in.wait_sent()


def front_call(x, cot, wp, gains, biases, ids, w_router, w_in, quarter, local_heads):
    n_dp, n_t = w_in.shape[0], lax.axis_size("tensor")
    rows, width = x.shape
    share, wide = wp.shape
    anywhere = pl.BlockSpec(memory_space=pl.ANY)
    vmem = pl.BlockSpec(memory_space=pltpu.VMEM)
    dma = pltpu.SemaphoreType.DMA

    def shape(*dims, kind=BF):
        return jax.ShapeDtypeStruct(dims, kind)

    group = (n_t, rows, width)
    pairs = w_in.shape[1]
    slots = (n_dp, pairs, 2 * quarter, width)
    return pl.pallas_call(
        lambda *refs: front_kernel(local_heads, *refs),
        out_shape=(
            shape(*group), shape(*group), shape(n_t, rows, width // 3), shape(n_dp, share, wide),
            shape(*slots), shape(rows, width, kind=F32), shape(n_dp, pairs * quarter, width),
            shape(n_dp, pairs * quarter, 1, kind=F32), shape(n_t, 2, rows, kind=F32),
            shape(*w_in.shape),
        ),
        in_specs=[vmem, vmem, anywhere, vmem, vmem, vmem, vmem, anywhere],
        out_specs=(anywhere,) * 5 + (vmem,) * 4 + (anywhere,),
        scratch_shapes=[pltpu.VMEM(group, BF)] * 4
        + [
            pltpu.VMEM((n_t, rows, width // 3), BF),
            pltpu.VMEM((n_dp, share, wide), BF),
            pltpu.VMEM(group, BF),
            pltpu.VMEM((n_t - 1, rows, width), BF),
            pltpu.VMEM(slots, BF),
        ]
        + [dma((n_dp,))] * 4
        + [dma((3, 3)), dma((3, 3)), dma((3,)), dma((3,)), dma((5,))],
        cost_estimate=pl.CostEstimate(
            flops=4 * n_t * rows * width * wide, bytes_accessed=400_000_000, transcendentals=0
        ),
        compiler_params=pltpu.CompilerParams(
            collective_id=2, has_side_effects=True, vmem_limit_bytes=50 * 1024 * 1024
        ),
        name="front",
    )(x, cot, wp, gains, biases, ids, w_router, w_in)


def back_kernel(
    local_heads, experts,
    came_ref, cots_ref, gate_ref, slot_ref, middle_ref, x_ref, cot_ref, gains_ref, biases_ref, wr_ref,
    a1_ref, three_ref, mixed_ref, w_ref, min_ref, mexp_ref, gin_ref, gexp_ref,
    output_ref, input_grad_ref, attn_ref, small_ref, min_out, mexp_out, gin_out, gexp_out,
    tok, cols, tok_landed, gm, part, landed, grads, sum_three, sum_out, shares,
    in_send, in_recv, exp_send, exp_recv, at_send, at_recv,
    ag_send, ag_recv, tok_send, tok_recv, sum_send, sum_recv,
):
    n_dp, share, wide = w_ref.shape
    n_t, rows, width = a1_ref.shape
    third = width // 3
    d, t = lax.axis_index("dp"), lax.axis_index("tensor")
    greet(n_dp, d, t)
    bulks = [
        Exchange(min_ref, min_out, in_send, in_recv, d, t),
        Exchange(mexp_ref, mexp_out, exp_send, exp_recv, d, t),
    ]
    for bulk in bulks:
        bulk.start()

    pairs, quarter = came_ref.shape[1], came_ref.shape[2] // 2
    held = pairs * quarter

    @pl.loop(0, n_dp)
    def _(host):
        at = pl.ds(pl.multiple_of(host * held, held), held)
        came = [came_ref[host, e].astype(F32) for e in range(pairs)]
        slot_out = jnp.concatenate([block[:quarter] for block in came], axis=0)
        row_grad = jnp.concatenate([block[quarter:] for block in came], axis=0)
        gate_grad = jnp.sum(cots_ref[host].astype(F32) * slot_out, axis=1, keepdims=True)
        lane = lax.broadcasted_iota(jnp.int32, (held, 128), 1) - host * pairs
        row = lax.broadcasted_iota(jnp.int32, (held, 128), 0)
        named = (row >= lane * quarter) & (row < (lane + 1) * quarter)
        cols[at, :width] = (gate_ref[host] * slot_out).astype(BF)
        cols[at, width : 2 * width] = row_grad.astype(BF)
        cols[at, 2 * width :] = jnp.where(
            named, jnp.broadcast_to(gate_grad, named.shape), 0.0
        ).astype(BF)

    tokens = Scatter(lambda r: tok.at[t ^ r], tok_landed, tok_send, tok_recv, d, t)
    number = lax.broadcasted_iota(jnp.int32, (cols.shape[0], rows), 0).astype(F32)
    for r in reversed(range(n_t)):
        image = t ^ r
        picks = [slot_ref[image, k : k + 1, :] == number for k in range(2)]
        spread = jnp.where(picks[0] | picks[1], 1.0, 0.0).astype(BF)
        tok[image] = dot(spread, cols[...], 0, 0).astype(BF)
        if r > 0:
            tokens.send(r)
    middle = middle_ref[...]
    gain_two = gains_ref[1:2, :]
    normed_two, inverse_two = layer_norm_parts(middle)
    act_two = only_tokens(normed_two * gain_two + biases_ref[1:2, :]).astype(BF)
    logits = dot(act_two, wr_ref[...], 1, 0)
    logits = jnp.where(lax.broadcasted_iota(jnp.int32, logits.shape, 1) < experts, logits, -1e30)
    expo = jnp.exp(logits - jnp.max(logits, axis=-1, keepdims=True))
    probs = expo / jnp.sum(expo, axis=-1, keepdims=True)
    total = tokens.total()
    output_ref[...] = (middle + total[:, :width]).astype(BF)
    grad_probs = total[:, 2 * width :]
    grad_logits = probs * (grad_probs - jnp.sum(probs * grad_probs, axis=-1, keepdims=True))
    grad_logits = only_tokens(grad_logits).astype(BF)
    second_grad = only_tokens(total[:, width : 2 * width]) + dot(grad_logits, wr_ref[...], 1, 1)
    grad_middle, gain_two_grad, bias_two_grad = norm_back(
        second_grad, normed_two, inverse_two, gain_two
    )
    grad_middle = only_tokens(grad_middle + cot_ref[...].astype(F32))
    input_grad_ref[...] = grad_middle
    gm[t] = grad_middle.astype(BF)
    gather = Gather(gm, ag_send, ag_recv, d, t)
    gather.start()
    small_ref[...] = jnp.zeros_like(small_ref)
    small_ref[1:2, :] = gain_two_grad
    small_ref[3:4, :] = bias_two_grad
    small_ref[4 : 4 + experts, :] = dot(grad_logits, act_two, 0, 0)[:experts]
    sum_three[...] = jnp.zeros_like(sum_three)
    sum_out[...] = jnp.zeros_like(sum_out)
    gather.pass_on()
    gather.finish()

    sums = Scatter(lambda r: part.at[r], landed, sum_send, sum_recv, d, t)
    for r in reversed(range(n_t)):
        image = t ^ r
        every = w_ref[...].reshape(n_dp * share, wide)
        grad_rows = gm[image]
        qkv = three_ref[image]
        query, key, value = [qkv[:, s * third : (s + 1) * third] for s in range(3)]
        grad_mixed = dot(grad_rows, every[:, width:], 1, 0).astype(BF)
        grad_query = jnp.zeros((rows, third), F32)
        grad_key = jnp.zeros((rows, third), F32)
        grad_value = jnp.zeros((rows, third), F32)
        for head in range(local_heads):
            head_weights = head_probs(query, key, head)
            grad_head = of_head(grad_mixed, head)
            grad_weights = dot(grad_head, value, 1, 1)
            delta = jnp.sum(head_weights * grad_weights, axis=-1, keepdims=True)
            grad_scores = (head_weights * (grad_weights - delta)).astype(BF)
            grad_query = grad_query + dot(grad_scores, of_head(key, head), 1, 0)
            grad_key = grad_key + dot(grad_scores, of_head(query, head), 0, 0)
            grad_value = grad_value + dot(head_weights.astype(BF), grad_head, 0, 0)
        grad_three = jnp.concatenate(
            [
                (grad_query * HD ** (-0.5)).astype(BF),
                (grad_key * HD ** (-0.5)).astype(BF),
                grad_value.astype(BF),
            ],
            axis=1,
        )
        part[r] = dot(grad_three, every[:, :width], 1, 1).astype(BF)
        if r > 0:
            sums.send(r)
        sum_three[...] += dot(a1_ref[image], grad_three, 0, 0)
        sum_out[...] += dot(grad_rows, mixed_ref[image], 0, 0)
    grads[:, :, :width] = sum_three[...].astype(BF).reshape(n_dp, share, width)
    grads[:, :, width:] = sum_out[...].astype(BF).reshape(n_dp, share, third)
    over_y = [
        remote(
            grads.at[d ^ 1 ^ (2 * i)], shares.at[i], at_send.at[i], at_recv.at[i], (d ^ 1, t)
        )
        for i in range(4)
    ]
    along_z = [
        remote(
            shares.at[i], shares.at[4 + i], at_send.at[4 + i], at_recv.at[4 + i], (d ^ (2 * i), t)
        )
        for i in range(1, 4)
    ]
    for copy in over_y:
        copy.start()

    for i in (2, 3, 1, 0):
        over_y[i].wait_recv()
        shares[i] = (shares[i].astype(F32) + grads[d ^ (2 * i)].astype(F32)).astype(BF)
        if i > 0:
            along_z[i - 1].start()

    first_grad = only_tokens(sums.total())
    normed_one, inverse_one = layer_norm_parts(x_ref[...].astype(F32))
    grad_in, gain_one_grad, bias_one_grad = norm_back(
        first_grad, normed_one, inverse_one, gains_ref[0:1, :]
    )
    input_grad_ref[...] += grad_in
    small_ref[0:1, :] = gain_one_grad
    small_ref[2:3, :] = bias_one_grad
    total = shares[0].astype(F32)
    for i in range(1, 4):
        along_z[i - 1].wait_recv()
        total = total + shares[4 + i].astype(F32)
    attn_ref[...] = total
    for copy in over_y + along_z:
        copy.wait_send()
    gather.wait_sent()
    tokens.wait_sent()
    sums.wait_sent()
    for bulk in bulks:
        bulk.finish()
        bulk.wait_sent()


def back_call(
    came, cots, gate, slot, middle, x, cot, gains, biases, w_router, a1, three, mixed, w,
    m_in, m_exp, g_in, g_exp, local_heads, experts,
):
    n_dp, share, wide = w.shape
    n_t, rows, width = a1.shape
    anywhere = pl.BlockSpec(memory_space=pl.ANY)
    vmem = pl.BlockSpec(memory_space=pltpu.VMEM)
    dma = pltpu.SemaphoreType.DMA
    small_rows = -(-(4 + experts) // 8) * 8
    cols = 2 * width + 128
    return pl.pallas_call(
        lambda *refs: back_kernel(local_heads, experts, *refs),
        out_shape=(
            jax.ShapeDtypeStruct((rows, width), BF),
            jax.ShapeDtypeStruct((rows, width), F32),
            jax.ShapeDtypeStruct((share, wide), F32),
            jax.ShapeDtypeStruct((small_rows, width), F32),
        )
        + (jax.ShapeDtypeStruct(m_exp.shape, BF),) * 4,
        in_specs=[vmem] * 14 + [anywhere] * 4,
        out_specs=(vmem,) * 4 + (anywhere,) * 4,
        input_output_aliases={16: 6, 17: 7},
        scratch_shapes=[
            pltpu.VMEM((n_t, rows, cols), BF),
            pltpu.VMEM((experts * came.shape[2] // 2, cols), BF),
            pltpu.VMEM((n_t - 1, rows, cols), BF),
            pltpu.VMEM((n_t, rows, width), BF),
            pltpu.VMEM((n_t, rows, width), BF),
            pltpu.VMEM((n_t - 1, rows, width), BF),
            pltpu.VMEM((n_dp, share, wide), BF),
            pltpu.VMEM((width, width), F32),
            pltpu.VMEM((width, width // 3), F32),
            pltpu.VMEM((n_dp, share, wide), BF),
        ]
        + [dma((n_dp,))] * 6
        + [dma((3,))] * 6,
        cost_estimate=pl.CostEstimate(
            flops=20 * n_t * rows * width * wide, bytes_accessed=300_000_000, transcendentals=0
        ),
        compiler_params=pltpu.CompilerParams(
            collective_id=3, has_side_effects=True, vmem_limit_bytes=56 * 1024 * 1024
        ),
        name="back",
    )(
        came, cots, gate, slot, middle, x, cot, gains, biases, w_router, a1, three, mixed, w,
        m_in, m_exp, g_in, g_exp,
    )


def last_kernel(
    min_ref, mexp_ref, gin_ref, gexp_ref, pay_ref,
    ortho_ref, gin_out, gexp_out, all_out, small_ref,
    held, grown, moments, current, pays, alls, square, rest, poly, size,
    load_sem, pay_send, pay_recv, in_send, in_recv, exp_send, exp_recv,
    mat_send, mat_recv, ag_send, ag_recv, out_sem,
):
    n_dp, n_experts, share, width = gin_ref.shape
    n_t = moments.shape[0]
    d, t = lax.axis_index("dp"), lax.axis_index("tensor")
    loads = []
    for q in range(n_t):
        kind, e = divmod(q, n_experts)
        for n, (source, target) in enumerate(
            (((min_ref, mexp_ref)[kind], held), ((gin_ref, gexp_ref)[kind], grown))
        ):
            loads.append(
                pltpu.make_async_copy(source.at[:, e], target.at[q], load_sem.at[n, q])
            )
    for load in loads:
        load.start()
    barrier = pltpu.get_barrier_semaphore()
    pl.semaphore_signal(barrier, inc=1, device_id=(d, t ^ 3), device_id_type=MESH)
    greet(n_dp, d, t, 1)

    pay = Spread(pay_ref, pays, pay_send, pay_recv, d, t)
    pay.start()
    bulks = [
        Exchange(gin_ref, gin_out, in_send, in_recv, d, t),
        Exchange(gexp_ref, gexp_out, exp_send, exp_recv, d, t),
    ]
    for bulk in bulks:
        bulk.start()
    for load in loads:
        load.wait()

    @pl.loop(0, n_t)
    def _(q):
        for k in range(n_dp):
            moments[q, k] = (DECAY * held[q, k].astype(F32) + grown[q, k].astype(F32)).astype(BF)

    def matrix(step):
        return remote(
            moments.at[t ^ step], current.at[step],
            mat_send.at[step], mat_recv.at[step], (d, t ^ step),
        )

    own_matrix = pltpu.make_async_copy(moments.at[t], current.at[0], mat_recv.at[0])
    own_matrix.start()
    for step in (2, 3, 1):
        matrix(step).start()

    pay.finish()
    total = jnp.zeros((pays.shape[1] - share, width), F32)
    for k in range(n_dp):
        alls[t, k * share : (k + 1) * share] = pays[k, :share]
        total = total + pays[k, share:].astype(F32)
    alls[t, n_dp * share :] = total.astype(BF)
    gather = Gather(alls, ag_send, ag_recv, d, t)

    ortho = Ortho(current, square, rest, poly, size)
    ortho.clear()
    own_matrix.wait()
    ortho.add_square(0)
    matrix(1).wait_recv()
    ortho.add_square(1)
    gather.start()
    for step in (2, 3):
        matrix(step).wait_recv()
        ortho.add_square(step)
    ortho.steps()
    gather.pass_on()
    for b in range(n_t):
        block = ortho.grown(b)
        for k in range(n_dp):
            ortho_ref[k, t ^ b] = block[k * share : (k + 1) * share]
    gather.finish()
    out = pltpu.make_async_copy(alls, all_out, out_sem)
    out.start()
    small = jnp.zeros(small_ref.shape, F32)
    for b in range(n_t):
        small = small + alls[b, n_dp * share :].astype(F32)
    small_ref[...] = small
    out.wait()
    gather.wait_sent()
    for step in range(1, n_t):
        matrix(step).wait_send()

    pay.wait_sent()
    for bulk in bulks:
        bulk.finish()
        bulk.wait_sent()


def last_call(m_in, m_exp, g_in, g_exp, pay):
    n_dp, n_experts, share, width = g_in.shape
    n_t = lax.axis_size("tensor")
    anywhere = pl.BlockSpec(memory_space=pl.ANY)
    vmem = pl.BlockSpec(memory_space=pltpu.VMEM)
    dma = pltpu.SemaphoreType.DMA
    mats = pltpu.VMEM((n_t, n_dp, share, width), BF)
    every = (n_t, n_dp * share + pay.shape[0] - share, width)
    bulk = jax.ShapeDtypeStruct(g_in.shape, BF)
    return pl.pallas_call(
        last_kernel,
        out_shape=(
            jax.ShapeDtypeStruct((n_dp, n_t, share, width), BF),
            bulk,
            bulk,
            jax.ShapeDtypeStruct(every, BF),
            jax.ShapeDtypeStruct((pay.shape[0] - share, width), F32),
        ),
        in_specs=[anywhere] * 5,
        out_specs=(vmem, anywhere, anywhere, anywhere, vmem),
        scratch_shapes=[
            mats,
            mats,
            mats,
            mats,
            pltpu.VMEM((n_dp,) + pay.shape, BF),
            pltpu.VMEM(every, BF),
            pltpu.VMEM((width, width), F32),
            pltpu.VMEM((width, width), BF),
            pltpu.VMEM((width, width), BF),
            pltpu.VMEM((1, 1), F32),
            dma((2, n_t)),
        ]
        + [dma((n_dp,))] * 6
        + [dma((n_t,))] * 2
        + [dma((3,))] * 2
        + [dma],
        cost_estimate=pl.CostEstimate(
            flops=80 * width * width * width, bytes_accessed=300_000_000, transcendentals=0
        ),
        compiler_params=pltpu.CompilerParams(
            collective_id=4, has_side_effects=True, vmem_limit_bytes=58 * 1024 * 1024
        ),
        name="last",
    )(m_in, m_exp, g_in, g_exp, pay)


def local(
    inputs,
    cotangent,
    expert_ids,
    layer_norm_gains,
    layer_norm_biases,
    norm_moment,
    w_qkv,
    w_attn_out,
    w_router,
    w_in,
    w_exp_out,
    m_qkv,
    m_attn_out,
    m_router,
    m_in,
    m_exp_out,
):
    rows, width = inputs.shape
    group_rows, top_count = expert_ids.shape
    experts, share, hidden = w_in.shape
    head_cols = w_attn_out.shape[0]
    n_dp = lax.axis_size("dp")
    n_t = lax.axis_size("tensor")
    t_index = lax.axis_index("tensor")
    d_index = lax.axis_index("dp")
    per_host = experts // n_dp
    rows_pad = -(-rows // 16) * 16
    quarter = -(-(-(-CAP // n_t)) // 8) * 8
    third = width // 3

    def padded(block):
        return jnp.pad(block, ((0, rows_pad - rows), (0, 0)))

    def by_host(shard):
        return shard.reshape(n_dp, per_host, share, hidden)

    def pack_attention(three, out):
        return jnp.concatenate([three[0], three[1], three[2], out.T], axis=1)

    blocks = pack_attention(w_qkv, w_attn_out).reshape(share, 4, head_cols)
    blocks = jnp.pad(blocks, ((0, 0), (0, 0), (0, third - head_cols))).reshape(share, 4 * third)
    x_pad, cot_pad = padded(inputs), padded(cotangent)
    ids = jnp.pad(
        expert_ids.reshape(n_t, rows, top_count).transpose(0, 2, 1),
        ((0, 0), (0, 0), (0, rows_pad - rows)),
        constant_values=-1,
    )
    act_one_group, three, mixed, attn_weights, slot_pair, middle, cots, gate, slot, sent_in = front_call(
        x_pad,
        cot_pad,
        blocks,
        layer_norm_gains,
        layer_norm_biases,
        ids,
        w_router.T,
        by_host(w_in),
        quarter,
        head_cols // HD,
    )
    came, in_grad_parts, exp_grad_parts = experts_call(
        slot_pair, sent_in, by_host(jnp.swapaxes(w_exp_out, 1, 2))
    )

    results = back_call(
        came,
        cots,
        gate,
        slot,
        middle,
        x_pad,
        cot_pad,
        layer_norm_gains,
        layer_norm_biases,
        jnp.pad(w_router, ((0, 0), (0, 128 - experts))),
        act_one_group,
        three,
        mixed,
        attn_weights,
        by_host(m_in.astype(BF)),
        by_host(jnp.swapaxes(m_exp_out.astype(BF), 1, 2)),
        in_grad_parts,
        exp_grad_parts,
        head_cols // HD,
        experts,
    )
    output, input_grad, attn_sum, small_part = results[:4]
    sent_m_in, sent_m_exp, in_grad_parts, exp_grad_parts = results[4:]
    output, input_grad = output[:rows], input_grad[:rows]
    attn_sum = attn_sum.reshape(share, 4, third)[:, :, :head_cols].reshape(share, width)

    attn_moment = DECAY * pack_attention(m_qkv, m_attn_out) + attn_sum
    attn_blocks = attn_moment.reshape(share, 4, head_cols)
    qkv_moment_new = attn_blocks[:, :3].transpose(1, 0, 2)
    attn_out_moment_new = attn_blocks[:, 3].T
    pay_rows = -(-small_part.shape[0] // 16) * 16
    small_part = jnp.pad(small_part, ((0, pay_rows - small_part.shape[0]), (0, 0)))
    pay = jnp.concatenate([attn_moment, small_part], 0).astype(BF)

    ortho, in_grad, exp_grad, gathered, small = last_call(
        sent_m_in, sent_m_exp, in_grad_parts, exp_grad_parts, pay
    )
    ortho = lax.all_to_all(
        ortho.reshape(n_dp * n_t, share, hidden),
        ("dp", "tensor"),
        split_axis=0,
        concat_axis=0,
        tiled=True,
    )
    ortho = ortho.reshape(n_dp, 2, per_host, share, hidden).transpose(1, 0, 2, 3, 4)
    ortho_in, ortho_exp = ortho.reshape(2, experts, share, hidden)
    in_grad = in_grad.reshape(experts, share, hidden)
    exp_grad = exp_grad.reshape(experts, share, hidden)

    three_cols = 3 * head_cols
    last = gathered[n_t - 1, :width]
    packed_three = jnp.stack(
        [
            jnp.concatenate(
                [
                    gathered[b, :width, :three_cols],
                    last[:, b * head_cols : (b + 1) * head_cols],
                ],
                axis=1,
            )
            for b in range(3)
        ]
    )
    packed_out = jnp.concatenate([gathered[t, :width, three_cols:] for t in range(n_t)], axis=1)
    last_three, poly_three = ortho_call(packed_three)
    last_out, poly_out = ortho_call(packed_out[None])
    own_cols = jnp.where(
        t_index == n_t - 1,
        jnp.concatenate([last_three[b, :, three_cols:] for b in range(3)], axis=1),
        lax.dynamic_index_in_dim(last_three, jnp.minimum(t_index, 2), 0, False)[:, :three_cols],
    )
    own_rows = lax.dynamic_slice_in_dim(poly_three, d_index * share, share, 0)
    own_three = mm("ri,ic->rc", own_rows, own_cols)
    own_rows = lax.dynamic_slice_in_dim(poly_out, d_index * share, share, 0)
    own_cols = lax.dynamic_slice_in_dim(last_out[0], t_index * head_cols, head_cols, 1)
    own_out = mm("ri,ic->rc", own_rows, own_cols)
    own_qkv = own_three.reshape(share, 3, head_cols).transpose(1, 0, 2)
    qkv_new = w_qkv.astype(F32) - math.sqrt(3.0) * own_qkv
    attn_out_new = w_attn_out.astype(F32) - own_out.T

    norm_moment_new = DECAY * norm_moment + small[:4]
    norm_new = (
        jnp.concatenate([layer_norm_gains, layer_norm_biases], 0) - VEC_RATE * norm_moment_new
    )
    router_moment_turned = DECAY * m_router.T + small[4 : 4 + experts]
    router_moment_new = router_moment_turned.T
    router_new = w_router.astype(F32) - local_orthogonalize(router_moment_turned).T

    in_moment_new = DECAY * m_in + in_grad.astype(F32)
    exp_out_moment_new = DECAY * m_exp_out + jnp.swapaxes(exp_grad, 1, 2).astype(F32)
    in_new = w_in.astype(F32) - math.sqrt(max(1.0, FF / D)) * ortho_in.astype(F32)
    exp_out_new = w_exp_out.astype(F32) - jnp.swapaxes(ortho_exp, 1, 2).astype(F32)
    return (
        output,
        input_grad,
        norm_moment_new,
        norm_new,
        qkv_moment_new,
        qkv_new,
        attn_out_moment_new,
        attn_out_new,
        router_moment_new,
        router_new,
        in_moment_new,
        in_new,
        exp_out_moment_new,
        exp_out_new,
    )


def general(
    inputs,
    cotangent,
    expert_ids,
    layer_norm_gains,
    layer_norm_biases,
    norm_moment,
    w_qkv,
    w_attn_out,
    w_router,
    w_in,
    w_exp_out,
    m_qkv,
    m_attn_out,
    m_router,
    m_in,
    m_exp_out,
):
    rows, width = inputs.shape
    group_rows, top_count = expert_ids.shape
    experts, share, hidden = w_in.shape
    head_cols = w_attn_out.shape[0]
    heads = width // HD
    n_dp = lax.axis_size("dp")
    n_t = lax.axis_size("tensor")
    t_index = lax.axis_index("tensor")
    d_index = lax.axis_index("dp")
    per_host = max(1, experts // n_dp)
    copies = max(1, n_dp // experts)
    hosts = n_dp * per_host
    part = hidden // copies
    scale_qk = HD ** (-0.5)
    rows_pad = -(-rows // 16) * 16
    group_pad = n_t * rows_pad
    quarter = -(-(-(-CAP // n_t)) // 16) * 16
    slots = experts * quarter

    def padded(block):
        return jnp.pad(block, ((0, rows_pad - rows), (0, 0)))

    def group_of(block):
        return lax.all_gather(padded(block), "tensor", axis=0, tiled=True)

    def exchange(blocks, axis):
        return lax.all_to_all(blocks, axis, split_axis=0, concat_axis=0, tiled=True)

    def to_host(shard):
        parts = shard.reshape(experts, share, copies, part).transpose(0, 2, 1, 3)
        return exchange(parts.reshape(n_dp, per_host, share, part), "dp")

    def at_host(blocks):
        return blocks.transpose(1, 0, 2, 3).reshape(per_host, n_dp * share, part)

    def from_host(whole):
        blocks = whole.reshape(per_host, n_dp, share, part).transpose(1, 0, 2, 3)
        back = exchange(blocks, "dp").reshape(experts, copies, share, part)
        return back.transpose(0, 2, 1, 3).reshape(experts, share, copies * part)

    def pack_attention(three, out):
        return jnp.concatenate([three[0], three[1], three[2], out.T], axis=1)

    attn_weights = lax.all_gather(pack_attention(w_qkv, w_attn_out), "dp", axis=0, tiled=True)
    w_three, w_out_turned = attn_weights[:, : 3 * head_cols], attn_weights[:, 3 * head_cols :]
    w_exp_turned = jnp.swapaxes(w_exp_out, 1, 2)
    m_in_short = m_in.astype(BF)
    m_exp_short = jnp.swapaxes(m_exp_out.astype(BF), 1, 2)

    ids = expert_ids.reshape(n_t, rows, top_count)
    ids = jnp.pad(ids, ((0, 0), (0, rows_pad - rows), (0, 0)), constant_values=-1)
    ids = ids.reshape(group_pad, top_count)
    labels = lax.broadcasted_iota(jnp.int32, (group_pad, top_count, experts), 2)
    chosen = (ids[:, :, None] == labels).astype(F32)
    counted = jnp.sum(chosen, axis=1)
    earlier = (
        lax.broadcasted_iota(jnp.int32, (group_pad, group_pad), 0)
        > lax.broadcasted_iota(jnp.int32, (group_pad, group_pad), 1)
    ).astype(BF)
    before = mm("ts,se->te", earlier, counted.astype(BF))
    places = jnp.sum(before[:, None, :] * chosen, axis=2).astype(jnp.int32) - t_index * quarter
    mine = (places >= 0) & (places < quarter) & (ids >= 0)
    slot_of = jnp.where(mine, ids * quarter + places, -1)
    slot_rows = lax.broadcasted_iota(jnp.int32, (slots, group_pad), 0)
    picks = [slot_of[:, k][None, :] == slot_rows for k in range(top_count)]
    spread = sum(pick.astype(BF) for pick in picks)

    hidden_rows = inputs.astype(F32)
    first, first_normed, first_inverse = apply_layer_norm(
        hidden_rows, layer_norm_gains[0], layer_norm_biases[0]
    )
    act_one_group = group_of(first.astype(BF))
    cot_group = group_of(cotangent)
    images = rows // SEQ * n_t
    image_pad = group_pad // images

    def by_head(block):
        return block.reshape(images, image_pad, -1, HD)

    three = mm("td,dc->tc", act_one_group, w_three).astype(BF)
    query, key, value = [
        by_head(three[:, s * head_cols : (s + 1) * head_cols]) for s in range(3)
    ]
    scores = mm("bqhe,bkhe->bhqk", query, key) * scale_qk
    scores = jnp.where(lax.broadcasted_iota(jnp.int32, scores.shape, 3) < SEQ, scores, -1e30)
    expo = jnp.exp(scores - jnp.max(scores, axis=-1, keepdims=True))
    probs = expo / jnp.sum(expo, axis=-1, keepdims=True)
    probs_short = probs.astype(BF)
    mixed = mm("bhqk,bkhe->bqhe", probs_short, value).astype(BF).reshape(group_pad, head_cols)
    mixed = after(mixed, cot_group)
    attended = mm("te,de->td", mixed, w_out_turned).astype(BF)
    attended = lax.psum_scatter(attended, "tensor", scatter_dimension=0, tiled=True)
    middle = hidden_rows + attended[:rows].astype(F32)
    second, second_normed, second_inverse = apply_layer_norm(
        middle, layer_norm_gains[1], layer_norm_biases[1]
    )
    act_two = second.astype(BF)
    act_two_group = group_of(act_two)

    group_probs = jax.nn.softmax(mm("td,de->te", act_two_group, w_router), axis=-1)
    gates = jnp.sum(group_probs[:, None, :] * chosen, axis=2)
    gate_of_slot = sum(
        jnp.sum(jnp.where(pick, gates[:, k][None, :], 0.0), axis=1) for k, pick in enumerate(picks)
    )[:, None]
    slot_act = mm("st,td->sd", spread, act_two_group).astype(BF)
    cot_slot = mm("st,td->sd", spread, cot_group)
    slot_grad = (gate_of_slot * cot_slot).astype(BF)
    slot_pair = jnp.stack(
        [slot_act.reshape(experts, quarter, width), slot_grad.reshape(experts, quarter, width)], 1
    )
    if copies > 1:
        slot_pair = jnp.repeat(slot_pair, copies, axis=0)
    slot_pair = slot_pair.reshape(n_dp, per_host, 2, quarter, width)
    got = exchange(slot_pair, "dp")
    sent_in, sent_exp = to_host(w_in), to_host(w_exp_turned)
    sent_m_in, sent_m_exp = to_host(m_in_short), to_host(m_exp_short)
    host_in = at_host(sent_in)
    host_exp = at_host(sent_exp)
    in_grads, exp_grads, backs = [], [], []
    for e in range(per_host):
        e_rows, e_grad = [
            lax.all_gather(
                got[:, e, kind].reshape(n_dp * quarter, width), "tensor", axis=0, tiled=True
            )
            for kind in range(2)
        ]
        e_pre = mm("cd,df->cf", e_rows, host_in[e])
        normal = 0.5 * (1.0 + lax.erf(e_pre * INV_ROOT_TWO))
        slope = normal + e_pre * jnp.exp(-0.5 * e_pre * e_pre) * INV_ROOT_TWO_PI
        e_act = (e_pre * normal).astype(BF)
        e_grad_pre = (mm("cd,df->cf", e_grad, host_exp[e]) * slope).astype(BF)
        for part_sum in (
            mm("cf,df->cd", e_act, host_exp[e]),
            mm("cf,df->cd", e_grad_pre, host_in[e]),
        ):
            back = lax.psum_scatter(
                part_sum.astype(BF), "tensor", scatter_dimension=0, tiled=True
            )
            backs.append(back.reshape(n_dp, quarter, width))
        exp_grads.append(mm("cd,cf->df", e_grad, e_act))
        in_grads.append(mm("cd,cf->df", e_rows, e_grad_pre))
    host_in_grad, host_exp_grad = jnp.stack(in_grads), jnp.stack(exp_grads)

    back = jnp.stack(backs, axis=1)
    came = exchange(back, "dp").reshape(n_dp, per_host, 2, quarter, width)
    came = came.reshape(hosts // copies, copies, 2, quarter, width).astype(F32).sum(axis=1)
    moments = jnp.concatenate(
        [
            DECAY * at_host(sent_m_in).astype(F32) + host_in_grad,
            DECAY * at_host(sent_m_exp).astype(F32) + host_exp_grad,
        ],
        axis=0,
    ).astype(BF)
    in_grad = from_host(host_in_grad.astype(BF))
    exp_grad = from_host(host_exp_grad.astype(BF))
    members = [[e * copies + r for r in range(copies)] for e in range(n_dp // copies)]
    wide = lax.all_gather(moments, "tensor", axis=2, tiled=True)
    if copies > 1:
        wide = lax.all_gather(wide, "dp", axis=2, tiled=True, axis_index_groups=members)
    first_col = (lax.rem(d_index, copies) * n_t + t_index) * part
    own = [
        lax.dynamic_slice_in_dim(orthogonalize(wide[i]), first_col, part, 1)
        for i in range(2 * per_host)
    ]
    ortho = jnp.stack(own)

    slot_out = came[:, 0].reshape(slots, width)
    slot_row_grad = came[:, 1].reshape(slots, width).astype(BF)
    weighted = (gate_of_slot * slot_out).astype(BF)
    gate_grad_slot = jnp.sum(cot_slot * slot_out, axis=1)
    of_expert = (
        lax.broadcasted_iota(jnp.int32, (slots, 128), 0) // quarter
        == lax.broadcasted_iota(jnp.int32, (slots, 128), 1)
    )
    gate_grad_slot = jnp.where(of_expert, gate_grad_slot[:, None], 0.0).astype(BF)
    spread_cols = jnp.concatenate([weighted, slot_row_grad, gate_grad_slot], axis=1)
    token_part = mm("st,sc->tc", spread, spread_cols).astype(BF)
    token_sum = lax.psum_scatter(token_part, "tensor", scatter_dimension=0, tiled=True)
    token_sum = token_sum[:rows].astype(F32)
    output = (middle + token_sum[:, :width]).astype(BF)
    grad_probs = token_sum[:, 2 * width : 2 * width + experts]

    probs_local = jax.nn.softmax(mm("td,de->te", act_two, w_router), axis=-1)
    grad_logits = (
        probs_local * (grad_probs - jnp.sum(probs_local * grad_probs, axis=-1, keepdims=True))
    ).astype(BF)
    second_grad = token_sum[:, width : 2 * width] + mm("te,de->td", grad_logits, w_router)
    router_part = mm("td,te->ed", act_two, grad_logits)
    grad_mid_norm, gain_two_grad, bias_two_grad = norm_back(
        second_grad, second_normed, second_inverse, layer_norm_gains[1]
    )
    grad_middle = grad_mid_norm + cotangent.astype(F32)
    grad_mid_short = grad_middle.astype(BF)

    grad_mid_group = group_of(grad_mid_short)
    grad_heads = by_head(mm("td,de->te", grad_mid_group, w_out_turned).astype(BF))
    grad_weights = mm("bqhe,bkhe->bhqk", grad_heads, value)
    delta = jnp.sum(probs * grad_weights, axis=-1, keepdims=True)
    grad_scores = (probs * (grad_weights - delta)).astype(BF)
    grad_query = (mm("bhqk,bkhe->bqhe", grad_scores, key) * scale_qk).astype(BF)
    grad_key = (mm("bhqk,bqhe->bkhe", grad_scores, query) * scale_qk).astype(BF)
    grad_value = mm("bhqk,bqhe->bkhe", probs_short, grad_heads).astype(BF)
    grad_three = jnp.concatenate(
        [part.reshape(group_pad, head_cols) for part in (grad_query, grad_key, grad_value)], axis=1
    )
    first_grad = mm("tc,dc->td", grad_three, w_three).astype(BF)
    attn_grad = jnp.concatenate(
        [
            mm("td,tc->dc", act_one_group, grad_three).astype(BF),
            mm("td,tc->dc", grad_mid_group, mixed).astype(BF),
        ],
        axis=1,
    )
    attn_parts = exchange(attn_grad.reshape(n_dp, share, width), "dp")
    attn_sum = jnp.sum(attn_parts.astype(F32), axis=0)

    first_grad = lax.psum_scatter(first_grad, "tensor", scatter_dimension=0, tiled=True)
    grad_in_norm, gain_one_grad, bias_one_grad = norm_back(
        first_grad[:rows].astype(F32), first_normed, first_inverse, layer_norm_gains[0]
    )
    input_grad = grad_in_norm + grad_middle

    attn_moment = DECAY * pack_attention(m_qkv, m_attn_out) + attn_sum
    attn_blocks = attn_moment.reshape(share, 4, head_cols)
    qkv_moment_new = attn_blocks[:, :3].transpose(1, 0, 2)
    attn_out_moment_new = attn_blocks[:, 3].T
    vec_part = jnp.concatenate([gain_one_grad, gain_two_grad, bias_one_grad, bias_two_grad], 0)
    small_rows = -(-(4 + experts) // 8) * 8
    small_part = jnp.concatenate([vec_part, router_part], 0)
    small_part = jnp.pad(small_part, ((0, small_rows - 4 - experts), (0, 0)))
    gathered_dp = lax.all_gather(
        jnp.concatenate([attn_moment, small_part], 0).astype(BF), "dp", axis=0
    )
    small_part = jnp.sum(gathered_dp[:, share:].astype(F32), axis=0).astype(BF)
    gathered = jnp.concatenate([gathered_dp[:, :share].reshape(width, width), small_part], 0)
    gathered = lax.all_gather(gathered, "tensor", axis=0)
    small = jnp.sum(gathered[:, width:].astype(F32), axis=0)
    three_cols = 3 * head_cols
    last = gathered[n_t - 1, :width]
    packed_three = jnp.stack(
        [
            jnp.concatenate(
                [
                    gathered[b, :width, :three_cols],
                    last[:, b * head_cols : (b + 1) * head_cols],
                ],
                axis=1,
            )
            for b in range(3)
        ]
    )
    packed_out = jnp.concatenate([gathered[t, :width, three_cols:] for t in range(n_t)], axis=1)
    last_three, poly_three = ortho_call(packed_three)
    last_out, poly_out = ortho_call(packed_out[None])
    own_cols = jnp.where(
        t_index == n_t - 1,
        jnp.concatenate([last_three[b, :, three_cols:] for b in range(3)], axis=1),
        lax.dynamic_index_in_dim(last_three, jnp.minimum(t_index, 2), 0, False)[:, :three_cols],
    )
    own_rows = lax.dynamic_slice_in_dim(poly_three, d_index * share, share, 0)
    own_three = mm("ri,ic->rc", own_rows, own_cols)
    own_rows = lax.dynamic_slice_in_dim(poly_out, d_index * share, share, 0)
    own_cols = lax.dynamic_slice_in_dim(last_out[0], t_index * head_cols, head_cols, 1)
    own_out = mm("ri,ic->rc", own_rows, own_cols)
    own_qkv = own_three.reshape(share, 3, head_cols).transpose(1, 0, 2)
    qkv_new = w_qkv.astype(F32) - math.sqrt(3.0) * own_qkv
    attn_out_new = w_attn_out.astype(F32) - own_out.T

    norm_moment_new = DECAY * norm_moment + small[:4]
    norm_new = (
        jnp.concatenate([layer_norm_gains, layer_norm_biases], 0) - VEC_RATE * norm_moment_new
    )
    router_moment_turned = DECAY * m_router.T + small[4 : 4 + experts]
    router_moment_new = router_moment_turned.T
    router_new = w_router.astype(F32) - local_orthogonalize(router_moment_turned).T

    ortho_in, ortho_exp = from_host(ortho[:per_host]), from_host(ortho[per_host:])
    in_moment_new = DECAY * m_in + in_grad.astype(F32)
    exp_out_moment_new = DECAY * m_exp_out + jnp.swapaxes(exp_grad, 1, 2).astype(F32)
    in_new = w_in.astype(F32) - math.sqrt(max(1.0, FF / D)) * ortho_in.astype(F32)
    exp_out_new = w_exp_out.astype(F32) - jnp.swapaxes(ortho_exp, 1, 2).astype(F32)
    return (
        output,
        input_grad,
        norm_moment_new,
        norm_new,
        qkv_moment_new,
        qkv_new,
        attn_out_moment_new,
        attn_out_new,
        router_moment_new,
        router_new,
        in_moment_new,
        in_new,
        exp_out_moment_new,
        exp_out_new,
    )


def solution(mesh):
    both = P(("dp", "tensor"), None)
    cols = P(None, "dp", "tensor")
    turned = P(None, "tensor", "dp")
    in_specs = (
        both, both, P("dp", None), P(), P(), P(), cols, P("tensor", "dp"), P(), cols, turned,
        cols, P("tensor", "dp"), P(), cols, turned,
    )
    out_specs = (
        both, both, P(), P(), cols, cols, P("tensor", "dp"), P("tensor", "dp"), P(), P(),
        cols, cols, turned, turned,
    )
    n_dp, n_t = mesh.shape["dp"], mesh.shape["tensor"]
    whole = n_t == 4 and 2 * (EXPERTS // n_dp) == n_t and (D // n_dp) % 16 == 0
    step = local if whole else general
    return jax.shard_map(step, mesh=mesh, in_specs=in_specs, out_specs=out_specs, check_vma=False)
```

time: 2670 us -> 650 us (0.24)
  waiting for transfers between devices: 1070 us -> 20 us
  blocking collectives: 589 us -> 0 us
  Pallas kernels: 0 us -> 542 us
  matrix products: 472 us -> 4.88 us
  local copies, waits for them, and re-layouts: 350 us -> 29.8 us
  other arithmetic: 95.3 us -> 30.9 us
  starting transfers between devices: 62.8 us -> 15.2 us
    psum x5 -> x0, waiting for transfers between devices: 566 us -> none  [gram(): lax.psum(jnp.einsum('kic,kjc->kij', blocks, blocks, precision=HIGH).astyp...]
    pallas_call x0 -> x6, Pallas kernels: none -> 542 us  [the longest x1 178 us: experts_call(): pl.pallas_call(experts_kernel, out_shape=(jax.ShapeDtypeStruct(slots.shap...]
    dot_general x34 -> x2, matrix products: 463 us -> 1.7 us  [mm(): return jnp.einsum(spec, left, right, preferred_element_type=F32)]
    all_to_all x9 -> x1, waiting for transfers between devices: 371 us -> 20 us  [local(): lax.all_to_all(ortho.reshape(n_dp * n_t, share, hidden), ('dp', 'tensor')...]
    all_to_all x1 -> x0, blocking collectives: 259 us -> none  [local(): lax.all_to_all(outgoing, 'dp', split_axis=0, concat_axis=2, tiled=True)[0]]
    psum x1 -> x0, blocking collectives: 119 us -> none  [local(): vec_grad, router_grad = lax.psum((vec_part, router_part), ('dp', 'tensor'))]
    all_gather x2 -> x0, blocking collectives: 112 us -> none  [the longest x1 80.6 us: local(): lax.all_gather(w_qkv, 'dp', axis=1, tiled=True)]
    gather x15 -> x0, local copies, waits for them, and re-layouts: 106 us -> none  [the longest x3 19.3 us: local(): grad_at_slot = padded_grad[token_of_slot]]
  transfers between devices with their start and end apart: 25 -> 1, of which waited for: 15 -> 1; matrix products, arithmetic and copies ran while one was open for 18% -> 6% of each run, Pallas kernels for 0% -> 7%
where the time goes in v1:
time: 650 us; the launch traced here: 645 us
  Pallas kernels  542 us (83%)
  other arithmetic  30.9 us (5%)
  local copies, waits for them, and re-layouts  29.8 us (5%)
  waiting for transfers between devices  20 us (3%)
  starting transfers between devices  15.2 us (2%)
    pallas_call x1, Pallas kernels, experts_call(): pl.pallas_call(experts_kernel, out_shape=(jax.ShapeDtypeStruct(slots.shap...  178 us
    pallas_call x1, Pallas kernels, back_call(): pl.pallas_call(lambda *refs: back_kernel(local_heads, experts, *refs), ou...  127 us
    pallas_call x1, Pallas kernels, last_call(): pl.pallas_call(last_kernel, out_shape=(jax.ShapeDtypeStruct((n_dp, n_t, s...  116 us
    pallas_call x1, Pallas kernels, front_call(): pl.pallas_call(lambda *refs: front_kernel(local_heads, *refs), out_shape=...  73.3 us
    pallas_call x2, Pallas kernels, ortho_call(): pl.pallas_call(ortho_kernel, out_shape=(jax.ShapeDtypeStruct((count, n, w...  47.4 us
    all_to_all x1, waiting for transfers between devices, local(): lax.all_to_all(ortho.reshape(n_dp * n_t, share, hidden), ('dp', 'tensor')...  20 us
    all_to_all x1, starting transfers between devices, local(): lax.all_to_all(ortho.reshape(n_dp * n_t, share, hidden), ('dp', 'tensor')...  15.2 us
  transfers between devices with their start and end apart: 1, of which 1 were waited for; matrix products, arithmetic and copies ran while one was open for 6% of the time, Pallas kernels for 7%

profile of v1, /device:TPU:0, one launch (start us, length us, event | category | flops | bytes accessed | tf_op | source)
XLA Modules:
  0.0 644.6 jit_solution(5474684835165979358)
XLA Ops:
  0.7 1.1 copy.42
  1.8 0.9 fusion.27
  2.8 1.0 pad.24.refs_0_.refs_5_
  3.8 1.1 pad.25.refs_1_.refs_6_
  5.1 4.2 convert_element_type.59
  9.3 1.7 convert_element_type.60
  11.1 0.7 pad.28.refs_9_
  11.9 73.3 %front.1 = (bf16[4,208,768]{2,1,0:T(8,128)(2,1)}, bf16[4,208,768]{2,1,0:T(8,128)(2,1)}, bf16[4,208,256]{2,1,0:T(8,128)(2,1)S(1)}, bf16[8,96,1024]{2,1,0:T(8,128)...) custom-call(bf16[208,768]{1,0:T(8,128)(2,1)S(1)} %pad.24.refs_0_.ref, ...), custom_call_target="tpu_custom_call" | custom-call | flops 2617245696 | bytes 400000000 | tf_op jit(solution)/shard_map/front/pallas_call | solution.py:758
  85.2 0.9 copy-done.7
  86.2 0.8 copy-done.8
  87.0 0.8 copy-done.9
  87.8 0.7 copy-done.10
  88.5 0.6 copy-done.11
  89.1 178.3 %experts.1 = (bf16[8,2,80,768]{3,2,1,0:T(8,128)(2,1)}, bf16[8,2,96,768]{3,2,1,0:T(8,128)(2,1)}, bf16[8,2,96,768]{3,2,1,0:T(8,128)(2,1)}) custom-call(bf16[8,2,80,768]{3,2,1,0:T(8,128)(2,1)} %get-tuple-element.44.slots_ref, bf16[8,2,96,768]{3,2,1,0:T(8,128)(2,1)} %get-tuple-element.45.win_ref, bf16[8,2,96,768]{3,2,1,0:T(8,128)(2,1)} %bitcast.156), custom_call_target="tpu_custom_call" | custom-call | flops 120795955200 | bytes 400000000 | tf_op jit(solution)/shard_map/experts/pallas_call | solution.py:424
  267.4 126.6 %back.1 = (bf16[208,768]{1,0:T(8,128)(2,1)}, f32[208,768]{1,0:T(8,128)}, f32[96,1024]{1,0:T(8,128)}, f32[24,768]{1,0:T(8,128)}, bf16[8,2,96,768]{3,2,1,0:T(8,128...) custom-call(bf16[8,2,80,768]{3,2,1,0:T(8,128)(2,1)} %get-tuple-eleme, ...), custom_call_target="tpu_custom_call", output_to_operand_aliasing={{6}: (16, {}), {7}: (17, {})} | custom-call | flops 13086228480 | bytes 300000000 | tf_op jit(solution)/shard_map/back/pallas_call | solution.py:958
  394.0 1.2 reshape.100
  395.5 0.7 slice_bitcast_fusion.17
  396.4 0.7 fusion.28.pay_ref
  397.1 116.1 %last.1 = (bf16[8,4,96,768]{3,2,1,0:T(8,128)(2,1)}, bf16[8,2,96,768]{3,2,1,0:T(8,128)(2,1)}, bf16[8,2,96,768]{3,2,1,0:T(8,128)(2,1)}, bf16[4,800,768]{2,1,0:T(8,128)(2,1)}, f32[32,768]{1,0:T(8,128)}) custom-call(bf16[8,2,96,768]{3,2,1,0:T(8,128)(2,1)} %get-tuple-element.59.min_ref, bf16[8,2,96,768]{3,2,1,0:T(8,128)(2,1)} %get-tuple-element.60.mexp_ref, ...), custom_call_target="tpu_custom_call" | custom-call | flops 36238786560 | bytes 300000000 | tf_op jit(solution)/shard_map/last/pallas_call | solution.py:1100
  513.2 15.2 %all-to-all-start = ((bf16[32,96,768]{2,1,0:T(8,128)(2,1)}), bf16[32,96,768]{2,1,0:T(8,128)(2,1)}, u32[]{:S(2)}, u32[]{:S(2)}) async-start(bf16[32,96,768]{2,1,0:T(8,128)(2,1)} %bitcast.150), calls=%async_computation | async-start | bytes 9437184 | tf_op jit(solution)/shard_map/all_to_all | solution.py:1240
  528.4 3.0 slice_bitcast_fusion.3
  531.4 1.4 slice_bitcast_fusion
  532.8 2.1 multiply_reduce_fusion
  535.6 1.1 fusion.35
  536.7 1.5 maximum_bitcast_fusion.2
  538.2 1.6 maximum_bitcast_fusion
  539.8 2.0 pad_maximum_fusion.x_ref
  541.8 34.4 %orthogonalize.2 = (bf16[3,768,768]{2,1,0:T(8,128)(2,1)}, bf16[768,768]{1,0:T(8,128)(2,1)S(1)}) custom-call(bf16[3,768,768]{2,1,0:T(8,128)(2,1)} %pad_maximum_fusion.x_ref), custom_call_target="tpu_custom_call" | custom-call | flops 27179089920 | bytes 7077888 | tf_op jit(solution)/shard_map/orthogonalize/pallas_call | solution.py:189
  576.2 1.3 dynamic-slice_bitcast_fusion
  577.6 1.7 slice_bitcast_fusion.10
  579.3 0.6 convolution_multiply_fusion
  580.2 0.9 copy.54
  581.2 0.7 copy.55
  582.0 0.9 slice.90
  582.8 0.7 slice.89
  583.6 2.1 slice_bitcast_fusion.7
  588.7 1.4 maximum_subtract_fusion
  590.0 0.8 fusion.3
  590.9 13.1 %orthogonalize.3 = (bf16[1,768,768]{2,1,0:T(8,128)(2,1)S(1)}, bf16[768,768]{1,0:T(8,128)(2,1)S(1)}) custom-call(bf16[1,768,768]{2,1,0:T(8,128)(2,1)S(1)} %maximum_bitcast_fusion.3.x_ref), custom_call_target="tpu_custom_call" | custom-call | flops 9059696640 | bytes 2359296 | tf_op jit(solution)/shard_map/orthogonalize/pallas_call | solution.py:189
  603.9 1.1 convolution_subtract_fusion
  605.0 0.7 slice_bitcast_fusion.11
  605.8 4.8 convert_add_fusion
  610.6 3.1 fusion.1
  613.7 20.0 %all-to-all-done = bf16[32,96,768]{2,1,0:T(8,128)(2,1)} async-done(((bf16[32,96,768]{2,1,0:T(8,128)(2,1)}), bf16[32,96,768]{2,1,0:T(8,128)(2,1)}, u32[]{:S(2)}, u32[]{:S(2)}) %all-to-all-start) | async-done | bytes 4718624 | tf_op jit(solution)/shard_map/all_to_all | solution.py:1240
  633.7 2.7 copy.61
  637.0 1.5 copy-done.15
  638.5 2.9 bitcast_subtract_fusion
  641.4 2.9 fusion
  (97 shorter events, 4.9 us)
Async XLA Ops:
  0.6 4.3 copy-start.30
  1.7 0.9 copy-start.18
  3.8 8.1 %copy-start = (bf16[208,768]{1,0:T(8,128)(2,1)}, bf16[208,768]{1,0:T(8,128)(2,1)S(1)}, u32[]{:S(2)}) copy-start(bf16[208,768]{1,0:T(8,128)(2,1)S(1)} %pad.24.refs_0_.refs_5_) | copy-start | bytes 958468
  4.9 6.9 %copy-start.1 = (bf16[208,768]{1,0:T(8,128)(2,1)}, bf16[208,768]{1,0:T(8,128)(2,1)S(1)}, u32[]{:S(2)}) copy-start(bf16[208,768]{1,0:T(8,128)(2,1)S(1)} %pad.25.refs_1_.refs_6_) | copy-start | bytes 958468
  5.0 4.2 copy-start.12
  9.2 1.7 copy-start.2
  9.2 2.6 copy-start.3
  9.2 2.6 copy-start.5
  85.2 0.9 copy-start.7
  86.2 0.8 copy-start.8
  87.0 0.8 copy-start.9
  87.8 0.7 copy-start.10
  88.5 0.6 copy-start.11
  267.4 128.1 %copy-start.23 = (f32[3,96,192]{2,1,0:T(8,128)S(1)}, f32[3,96,192]{2,1,0:T(8,128)}, u32[]{:S(2)}) copy-start(f32[3,96,192]{2,1,0:T(8,128)} %param.27) | copy-start | bytes 663556
  394.0 2.2 copy-start.25
  394.0 2.3 copy-start.26
  395.2 118.0 %copy-start.13 = (f32[96,4,256]{2,1,0:T(4,128)}, f32[96,4,256]{2,1,0:T(4,128)S(1)}, u32[]{:S(2)}) copy-start(f32[96,4,256]{2,1,0:T(4,128)S(1)} %reshape.100) | copy-start | bytes 1179652
  513.2 120.5 %all-to-all-start = ((bf16[32,96,768]{2,1,0:T(8,128)(2,1)}), bf16[32,96,768]{2,1,0:T(8,128)(2,1)}, u32[]{:S(2)}, u32[]{:S(2)}) async-start(bf16[32,96,768]{2,1,0:T(8,128)(2,1)} %bitcast.150), calls=%async_computation | async-start | bytes 9437184 | tf_op jit(solution)/shard_map/all_to_all | solution.py:1240
  531.4 1.4 copy-start.27
  579.3 0.9 copy-start.19
  579.3 1.8 copy-start.14
  579.3 1.8 copy-start.21
  579.9 2.0 copy-start.20
  579.9 2.9 copy-start.22
  583.6 2.6 copy-start.28
  585.7 3.0 copy-start.4
  585.7 3.0 copy-start.6
  585.7 3.0 copy-start.29
  585.7 24.8 %slice-start.2 = ((s8[4718592]{0:T(1024)(128)(4,1)}), s8[524288]{0:T(1024)(128)(4,1)S(1)}, s32[]{:S(2)}) async-start(s8[4718592]{0:T(1024)(128)(4,1)} %bitcast.148), calls=%async_computation.3 | async-start | bytes 1048576
  590.0 15.7 %slice-start = ((s8[4718592]{0:T(1024)(128)(4,1)}), s8[4194304]{0:T(1024)(128)(4,1)S(1)}, s32[]{:S(2)}) async-start(s8[4718592]{0:T(1024)(128)(4,1)} %bitcast.146), calls=%async_computation.1 | async-start | bytes 8388608
  590.8 13.1 %copy-start.24 = (bf16[192,96]{1,0:T(8,128)(2,1)S(1)}, bf16[192,96]{1,0:T(8,128)(2,1)}, u32[]{:S(2)}) copy-start(bf16[192,96]{1,0:T(8,128)(2,1)} %param.23) | copy-start | bytes 110596
  590.8 14.9 %slice-start.1 = ((s8[4718592]{0:T(1024)(128)(4,1)}), s8[524288]{0:T(1024)(128)(4,1)S(1)}, s32[]{:S(2)}) async-start(s8[4718592]{0:T(1024)(128)(4,1)} %bitcast.146), calls=%async_computation.2 | async-start | bytes 1048576
  590.8 19.7 %slice-start.3 = ((s8[4718592]{0:T(1024)(128)(4,1)}), s8[4194304]{0:T(1024)(128)(4,1)S(1)}, s32[]{:S(2)}) async-start(s8[4718592]{0:T(1024)(128)(4,1)} %bitcast.148), calls=%async_computation.4 | async-start | bytes 8388608
  605.8 4.8 copy-start.17
  636.9 1.7 copy-start.15
  638.5 2.9 copy-start.16

commit v2 on v1

--- a/solution.py
+++ b/solution.py
@@ -333,9 +333,9 @@
         gexp_ref[:, e] = dot(rows_of[1], hidden_of[0], 0, 0).astype(BF).reshape(n_dp, share, width)
 
     pass_on(0)
-    send(1)
     pass_again(0)
     wait_second(0)
+    send(1)
     for e in range(n_experts):
         load(e).wait()
 
@@ -384,9 +384,9 @@
         def _():
             pass_on(1)
             weight_grads(0)
-            give_back(0)
             pass_again(1)
             wait_second(1)
+            give_back(0)
 
         @pl.when(step == 2 * n_t - 1)
         def _():

time: 650 us -> 642 us (0.988)
  Pallas kernels: 542 us -> 532 us
    pallas_call x1, Pallas kernels: 178 us -> 167 us  [experts_call(): pl.pallas_call(experts_kernel, out_shape=(jax.ShapeDtypeStruct(slots.shap...]
where the time goes in v2:
time: 642 us; the launch traced here: 636 us
  Pallas kernels  532 us (83%)
  other arithmetic  30.9 us (5%)
  local copies, waits for them, and re-layouts  29.8 us (5%)
  waiting for transfers between devices  20 us (3%)
  starting transfers between devices  16.2 us (3%)
    pallas_call x1, Pallas kernels, experts_call(): pl.pallas_call(experts_kernel, out_shape=(jax.ShapeDtypeStruct(slots.shap...  167 us
    pallas_call x1, Pallas kernels, back_call(): pl.pallas_call(lambda *refs: back_kernel(local_heads, experts, *refs), ou...  129 us
    pallas_call x1, Pallas kernels, last_call(): pl.pallas_call(last_kernel, out_shape=(jax.ShapeDtypeStruct((n_dp, n_t, s...  115 us
    pallas_call x1, Pallas kernels, front_call(): pl.pallas_call(lambda *refs: front_kernel(local_heads, *refs), out_shape=...  73.3 us
    pallas_call x2, Pallas kernels, ortho_call(): pl.pallas_call(ortho_kernel, out_shape=(jax.ShapeDtypeStruct((count, n, w...  47.4 us
    all_to_all x1, waiting for transfers between devices, local(): lax.all_to_all(ortho.reshape(n_dp * n_t, share, hidden), ('dp', 'tensor')...  20 us
    all_to_all x1, starting transfers between devices, local(): lax.all_to_all(ortho.reshape(n_dp * n_t, share, hidden), ('dp', 'tensor')...  16.2 us
  transfers between devices with their start and end apart: 1, of which 1 were waited for; matrix products, arithmetic and copies ran while one was open for 6% of the time, Pallas kernels for 7%

profile of v2, /device:TPU:0, one launch (start us, length us, event | category | flops | bytes accessed | tf_op | source)
XLA Modules:
  0.0 636.0 jit_solution(8438270655740672334)
XLA Ops:
  0.7 1.1 copy.42
  1.8 0.9 fusion.27
  2.8 1.0 pad.24.refs_0_.refs_5_
  3.8 1.1 pad.25.refs_1_.refs_6_
  5.1 4.2 convert_element_type.59
  9.3 1.7 convert_element_type.60
  11.1 0.7 pad.28.refs_9_
  11.9 73.3 %front.1 = (bf16[4,208,768]{2,1,0:T(8,128)(2,1)}, bf16[4,208,768]{2,1,0:T(8,128)(2,1)}, bf16[4,208,256]{2,1,0:T(8,128)(2,1)S(1)}, bf16[8,96,1024]{2,1,0:T(8,128)...) custom-call(bf16[208,768]{1,0:T(8,128)(2,1)S(1)} %pad.24.refs_0_.ref, ...), custom_call_target="tpu_custom_call" | custom-call | flops 2617245696 | bytes 400000000 | tf_op jit(solution)/shard_map/front/pallas_call | solution.py:758
  85.2 0.9 copy-done.7
  86.2 0.8 copy-done.8
  87.0 0.8 copy-done.9
  87.8 0.7 copy-done.10
  88.5 0.6 copy-done.11
  89.1 166.8 %experts.1 = (bf16[8,2,80,768]{3,2,1,0:T(8,128)(2,1)}, bf16[8,2,96,768]{3,2,1,0:T(8,128)(2,1)}, bf16[8,2,96,768]{3,2,1,0:T(8,128)(2,1)}) custom-call(bf16[8,2,80,768]{3,2,1,0:T(8,128)(2,1)} %get-tuple-element.44.slots_ref, bf16[8,2,96,768]{3,2,1,0:T(8,128)(2,1)} %get-tuple-element.45.win_ref, bf16[8,2,96,768]{3,2,1,0:T(8,128)(2,1)} %bitcast.156), custom_call_target="tpu_custom_call" | custom-call | flops 120795955200 | bytes 400000000 | tf_op jit(solution)/shard_map/experts/pallas_call | solution.py:424
  255.9 129.2 %back.1 = (bf16[208,768]{1,0:T(8,128)(2,1)}, f32[208,768]{1,0:T(8,128)}, f32[96,1024]{1,0:T(8,128)}, f32[24,768]{1,0:T(8,128)}, bf16[8,2,96,768]{3,2,1,0:T(8,128...) custom-call(bf16[8,2,80,768]{3,2,1,0:T(8,128)(2,1)} %get-tuple-eleme, ...), custom_call_target="tpu_custom_call", output_to_operand_aliasing={{6}: (16, {}), {7}: (17, {})} | custom-call | flops 13086228480 | bytes 300000000 | tf_op jit(solution)/shard_map/back/pallas_call | solution.py:958
  385.1 1.2 reshape.100
  386.6 0.7 slice_bitcast_fusion.17
  387.6 0.7 fusion.28.pay_ref
  388.2 115.4 %last.1 = (bf16[8,4,96,768]{3,2,1,0:T(8,128)(2,1)}, bf16[8,2,96,768]{3,2,1,0:T(8,128)(2,1)}, bf16[8,2,96,768]{3,2,1,0:T(8,128)(2,1)}, bf16[4,800,768]{2,1,0:T(8,128)(2,1)}, f32[32,768]{1,0:T(8,128)}) custom-call(bf16[8,2,96,768]{3,2,1,0:T(8,128)(2,1)} %get-tuple-element.59.min_ref, bf16[8,2,96,768]{3,2,1,0:T(8,128)(2,1)} %get-tuple-element.60.mexp_ref, ...), custom_call_target="tpu_custom_call" | custom-call | flops 36238786560 | bytes 300000000 | tf_op jit(solution)/shard_map/last/pallas_call | solution.py:1100
  503.6 16.2 %all-to-all-start = ((bf16[32,96,768]{2,1,0:T(8,128)(2,1)}), bf16[32,96,768]{2,1,0:T(8,128)(2,1)}, u32[]{:S(2)}, u32[]{:S(2)}) async-start(bf16[32,96,768]{2,1,0:T(8,128)(2,1)} %bitcast.150), calls=%async_computation | async-start | bytes 9437184 | tf_op jit(solution)/shard_map/all_to_all | solution.py:1240
  519.9 3.0 slice_bitcast_fusion.3
  522.9 1.4 slice_bitcast_fusion
  524.3 2.1 multiply_reduce_fusion
  527.1 1.1 fusion.35
  528.2 1.5 maximum_bitcast_fusion.2
  529.7 1.6 maximum_bitcast_fusion
  531.3 2.0 pad_maximum_fusion.x_ref
  533.3 34.4 %orthogonalize.2 = (bf16[3,768,768]{2,1,0:T(8,128)(2,1)}, bf16[768,768]{1,0:T(8,128)(2,1)S(1)}) custom-call(bf16[3,768,768]{2,1,0:T(8,128)(2,1)} %pad_maximum_fusion.x_ref), custom_call_target="tpu_custom_call" | custom-call | flops 27179089920 | bytes 7077888 | tf_op jit(solution)/shard_map/orthogonalize/pallas_call | solution.py:189
  567.7 1.3 dynamic-slice_bitcast_fusion
  569.0 1.7 slice_bitcast_fusion.10
  570.8 0.6 convolution_multiply_fusion
  571.7 0.9 copy.54
  572.7 0.7 copy.55
  573.5 0.9 slice.90
  574.3 0.7 slice.89
  575.1 2.1 slice_bitcast_fusion.7
  580.2 1.4 maximum_subtract_fusion
  581.5 0.8 fusion.3
  582.3 13.1 %orthogonalize.3 = (bf16[1,768,768]{2,1,0:T(8,128)(2,1)S(1)}, bf16[768,768]{1,0:T(8,128)(2,1)S(1)}) custom-call(bf16[1,768,768]{2,1,0:T(8,128)(2,1)S(1)} %maximum_bitcast_fusion.3.x_ref), custom_call_target="tpu_custom_call" | custom-call | flops 9059696640 | bytes 2359296 | tf_op jit(solution)/shard_map/orthogonalize/pallas_call | solution.py:189
  595.4 1.1 convolution_subtract_fusion
  596.5 0.7 slice_bitcast_fusion.11
  597.3 4.8 convert_add_fusion
  602.0 3.1 fusion.1
  605.1 20.0 %all-to-all-done = bf16[32,96,768]{2,1,0:T(8,128)(2,1)} async-done(((bf16[32,96,768]{2,1,0:T(8,128)(2,1)}), bf16[32,96,768]{2,1,0:T(8,128)(2,1)}, u32[]{:S(2)}, u32[]{:S(2)}) %all-to-all-start) | async-done | bytes 4718624 | tf_op jit(solution)/shard_map/all_to_all | solution.py:1240
  625.2 2.7 copy.61
  628.5 1.5 copy-done.15
  630.0 2.9 bitcast_subtract_fusion
  632.9 2.9 fusion
  (97 shorter events, 4.9 us)
Async XLA Ops:
  0.6 4.3 copy-start.30
  1.7 0.9 copy-start.18
  3.8 8.1 %copy-start = (bf16[208,768]{1,0:T(8,128)(2,1)}, bf16[208,768]{1,0:T(8,128)(2,1)S(1)}, u32[]{:S(2)}) copy-start(bf16[208,768]{1,0:T(8,128)(2,1)S(1)} %pad.24.refs_0_.refs_5_) | copy-start | bytes 958468
  4.9 6.9 %copy-start.1 = (bf16[208,768]{1,0:T(8,128)(2,1)}, bf16[208,768]{1,0:T(8,128)(2,1)S(1)}, u32[]{:S(2)}) copy-start(bf16[208,768]{1,0:T(8,128)(2,1)S(1)} %pad.25.refs_1_.refs_6_) | copy-start | bytes 958468
  5.0 4.2 copy-start.12
  9.2 1.7 copy-start.2
  9.2 2.6 copy-start.3
  9.2 2.6 copy-start.5
  85.2 0.9 copy-start.7
  86.2 0.8 copy-start.8
  87.0 0.8 copy-start.9
  87.8 0.7 copy-start.10
  88.5 0.6 copy-start.11
  255.9 130.7 %copy-start.23 = (f32[3,96,192]{2,1,0:T(8,128)S(1)}, f32[3,96,192]{2,1,0:T(8,128)}, u32[]{:S(2)}) copy-start(f32[3,96,192]{2,1,0:T(8,128)} %param.27) | copy-start | bytes 663556
  385.1 2.2 copy-start.25
  385.1 2.3 copy-start.26
  386.3 117.3 %copy-start.13 = (f32[96,4,256]{2,1,0:T(4,128)}, f32[96,4,256]{2,1,0:T(4,128)S(1)}, u32[]{:S(2)}) copy-start(f32[96,4,256]{2,1,0:T(4,128)S(1)} %reshape.100) | copy-start | bytes 1179652
  503.6 121.5 %all-to-all-start = ((bf16[32,96,768]{2,1,0:T(8,128)(2,1)}), bf16[32,96,768]{2,1,0:T(8,128)(2,1)}, u32[]{:S(2)}, u32[]{:S(2)}) async-start(bf16[32,96,768]{2,1,0:T(8,128)(2,1)} %bitcast.150), calls=%async_computation | async-start | bytes 9437184 | tf_op jit(solution)/shard_map/all_to_all | solution.py:1240
  522.9 1.4 copy-start.27
  570.8 0.9 copy-start.19
  570.8 1.8 copy-start.14
  570.8 1.8 copy-start.21
  571.4 2.0 copy-start.20
  571.4 2.9 copy-start.22
  575.1 2.6 copy-start.28
  577.1 3.0 copy-start.4
  577.2 3.0 copy-start.6
  577.2 3.0 copy-start.29
  577.2 24.8 %slice-start.2 = ((s8[4718592]{0:T(1024)(128)(4,1)}), s8[524288]{0:T(1024)(128)(4,1)S(1)}, s32[]{:S(2)}) async-start(s8[4718592]{0:T(1024)(128)(4,1)} %bitcast.148), calls=%async_computation.3 | async-start | bytes 1048576
  581.5 15.7 %slice-start = ((s8[4718592]{0:T(1024)(128)(4,1)}), s8[4194304]{0:T(1024)(128)(4,1)S(1)}, s32[]{:S(2)}) async-start(s8[4718592]{0:T(1024)(128)(4,1)} %bitcast.146), calls=%async_computation.1 | async-start | bytes 8388608
  582.3 13.1 %copy-start.24 = (bf16[192,96]{1,0:T(8,128)(2,1)S(1)}, bf16[192,96]{1,0:T(8,128)(2,1)}, u32[]{:S(2)}) copy-start(bf16[192,96]{1,0:T(8,128)(2,1)} %param.23) | copy-start | bytes 110596
  582.3 14.9 %slice-start.1 = ((s8[4718592]{0:T(1024)(128)(4,1)}), s8[524288]{0:T(1024)(128)(4,1)S(1)}, s32[]{:S(2)}) async-start(s8[4718592]{0:T(1024)(128)(4,1)} %bitcast.146), calls=%async_computation.2 | async-start | bytes 1048576
  582.3 19.7 %slice-start.3 = ((s8[4718592]{0:T(1024)(128)(4,1)}), s8[4194304]{0:T(1024)(128)(4,1)S(1)}, s32[]{:S(2)}) async-start(s8[4718592]{0:T(1024)(128)(4,1)} %bitcast.148), calls=%async_computation.4 | async-start | bytes 8388608
  597.3 4.8 copy-start.17
  628.4 1.7 copy-start.15
  630.0 2.9 copy-start.16
